TPU v7x, 512 devices: a whole 4x8x8 slice. The times are simulated.
512 devices in a mesh: dp: 32 (over y, x), head: 16 (over z, core).
Axes of the slice: x: 4, y: 8, z: 8, core: 2. Of those that a mesh axis runs over, the one named last changes fastest.
Arguments:
- queries: bfloat16 [64, 1024, 8192], P('dp', 'head'), may hold values from -6 to 6
- keys: bfloat16 [64, 1024, 1024], P('dp', 'head'), may hold values from -6 to 6
- values: bfloat16 [64, 1024, 1024], P('dp', 'head'), may hold values from -6 to 6
- segments: int32 [64, 1024], P('dp', 'head'), may hold values from 0 to 3, never falling along the last dimension, each value on 1 to 512 neighbouring positions
- modality: int32 [64, 1024], P('dp', 'head'), may hold values from 0 to 1, as said below
- q_scale: float32 [2, 64, 128], P(None, None, 'dp'), may hold values from 0.5 to 5
- q_shift: float32 [2, 64, 128], P(None, None, 'dp'), may hold values from -1.5 to 1.5
- k_scale: float32 [2, 8, 128], P(None, None, 'dp'), may hold values from 0.5 to 5
- k_shift: float32 [2, 8, 128], P(None, None, 'dp'), may hold values from -1.5 to 1.5
Outputs:
- attended: bfloat16 [64, 1024, 8192], P('dp', 'head')
Inputs may be any that keep to these rules, and one draw needn't show every extreme that they name: `modality`: constant over each aligned run of 128 positions of a pack.
All inputs are finite; a program needn't handle non-finite values.
Results may differ from a plain program's by a relative error of at most 0.012.
Values may be sent and summed in bfloat16 or wider, within the bound.
No kernel may reach another device: no remote copies, remote signals or barrier semaphores. Data moves between devices by JAX's collectives and lax.ppermute only.
A program may use at most 128 MiB of HBM per device.

v0:
```python
import jax
import jax.numpy as jnp
from jax import lax
from jax.sharding import PartitionSpec as P

KV = 8
HD = 128


def normalize(field, labels, scale, shift):
    packs, rows, width = field.shape
    count = scale.shape[1]
    heads = field.astype(jnp.float32).reshape(packs, rows, count, width // count)
    center = heads - jnp.mean(heads, axis=-1, keepdims=True)
    spread = jnp.mean(center * center, axis=-1, keepdims=True)
    picked = (labels == 1)[:, :, None, None]
    gains = jnp.where(picked, scale[1], scale[0])
    offsets = jnp.where(picked, shift[1], shift[0])
    normed = center * lax.rsqrt(spread + 1e-05) * gains + offsets
    return normed.astype(jnp.bfloat16).reshape(packs, rows, width)


def replicate(field, copies):
    packs, rows, width = field.shape
    spread_out = jnp.broadcast_to(
        field.reshape(packs, rows, width // HD, 1, HD), (packs, rows, width // HD, copies, HD)
    )
    return spread_out.reshape(packs, rows, width * copies)


def attend(query, key_rows, value_rows, query_seg, key_seg):
    packs, qrows, qwidth = query.shape
    krows = key_rows.shape[1]
    kv_local = key_rows.shape[2] // HD
    per_group = qwidth // HD // kv_local
    span = 512
    nblocks = qrows // span
    kpos = jnp.arange(krows, dtype=jnp.int32)

    def one_pack(item):
        qpart, kpart, vpart, qseg, kseg = item
        kheads = kpart.reshape(krows, kv_local, HD)
        vheads = vpart.reshape(krows, kv_local, HD)
        qblocks = qpart.reshape(nblocks, span, kv_local, per_group, HD)
        sblocks = qseg.reshape(nblocks, span)

        def one_block(inner):
            qheads, bseg, index = inner
            qpos = index * span + jnp.arange(span, dtype=jnp.int32)
            causal = kpos[None, :] <= qpos[:, None]
            scores = jnp.einsum(
                "skgd,tkd->kgst", qheads, kheads, preferred_element_type=jnp.float32
            ) * HD ** (-0.5)
            allowed = causal & (bseg[:, None] == kseg[None, :])
            scores = jnp.where(allowed, scores, -jnp.inf)
            top = jnp.max(scores, axis=-1, keepdims=True)
            weights = jnp.exp(scores - top)
            weights = (weights / jnp.sum(weights, axis=-1, keepdims=True)).astype(jnp.bfloat16)
            mixed = jnp.einsum(
                "kgst,tkd->skgd", weights, vheads, preferred_element_type=jnp.float32
            )
            return mixed.astype(jnp.bfloat16).reshape(span, qwidth)

        outputs = lax.map(one_block, (qblocks, sblocks, jnp.arange(nblocks, dtype=jnp.int32)))
        return outputs.reshape(qrows, qwidth)

    return lax.map(one_pack, (query, key_rows, value_rows, query_seg, key_seg))


def on_device(queries, keys, values, segments, modality, q_scale, q_shift, k_scale, k_shift):
    seg_whole = lax.all_gather(segments, "head", axis=1, tiled=True)
    qsc, qsh, ksc, ksh = (
        lax.all_gather(q_scale, "dp", axis=2, tiled=True),
        lax.all_gather(q_shift, "dp", axis=2, tiled=True),
        lax.all_gather(k_scale, "dp", axis=2, tiled=True),
        lax.all_gather(k_shift, "dp", axis=2, tiled=True),
    )
    width = lax.axis_size("head")
    q_normed = normalize(queries, modality, qsc, qsh)
    k_normed = normalize(keys, modality, ksc, ksh)
    copies = max(1, width // KV)
    q_local = lax.all_to_all(q_normed, "head", split_axis=2, concat_axis=1, tiled=True)
    k_local, v_local = (
        lax.all_to_all(
            replicate(k_normed, copies), "head", split_axis=2, concat_axis=1, tiled=True
        ),
        lax.all_to_all(replicate(values, copies), "head", split_axis=2, concat_axis=1, tiled=True),
    )
    mixed = attend(q_local, k_local, v_local, seg_whole, seg_whole)
    return lax.all_to_all(mixed, "head", split_axis=1, concat_axis=2, tiled=True)


def solution(mesh):
    placed = (
        P("dp", "head", None),
        P("dp", "head", None),
        P("dp", "head", None),
        P("dp", "head"),
        P("dp", "head"),
        P(None, None, "dp"),
        P(None, None, "dp"),
        P(None, None, "dp"),
        P(None, None, "dp"),
    )
    return jax.shard_map(
        on_device, mesh=mesh, in_specs=placed, out_specs=P("dp", "head", None), check_vma=False
    )
```

profile of v0, /device:TPU:1, one launch (start us, length us, event | category | flops | bytes accessed | tf_op | source)
XLA Modules:
  0.0 463.8 jit_solution(16637258646631427983)
XLA Ops:
  0.0 0.8 broadcast_compare_fusion
  0.8 1.0 copy.83
  2.5 0.7 copy.55
  3.2 32.3 %all_gather.18 = f32[2,8,128]{1,0,2:T(2,128)S(1)} all-gather(f32[2,8,4]{1,0,2:T(2,128)S(1)} %copy.55), channel_id=1, replica_groups=mesh['dp'=32,'head'=16] {'dp'}, dimensions={2}, use_global_device_ids=true | all-gather | bytes 8448 | tf_op jit(solution)/shard_map/all_gather | solution.py:75
  35.7 0.7 copy.58
  36.4 28.7 %all_gather.19 = f32[2,8,128]{1,0,2:T(2,128)S(1)} all-gather(f32[2,8,4]{1,0,2:T(2,128)S(1)} %copy.58), channel_id=1, replica_groups=mesh['dp'=32,'head'=16] {'dp'}, dimensions={2}, use_global_device_ids=true | all-gather | bytes 8448 | tf_op jit(solution)/shard_map/all_gather | solution.py:76
  65.4 0.5 add_convert_fusion
  65.9 1.1 copy.61
  67.0 1.8 broadcast_in_dim.116
  68.8 1.5 reshape.148
  70.3 27.4 %all-to-all-start.1 = ((bf16[16,2,8192]{2,1,0:T(2,128)(2,1)}), bf16[16,2,8192]{2,1,0:T(2,128)(2,1)}, u32[]{:S(2)}, u32[]{:S(2)}) async-start(bf16[16,2,8192]{2,1,0:T(2,128)(2,1)} %reshape.148), calls=%async_computation.1 | async-start | bytes 1048576 | tf_op jit(solution)/shard_map/all_to_all | solution.py:84
  97.7 6.9 %copy.46 = bf16[2,64,8192]{1,0,2:T(2,128)(2,1)} copy(bf16[2,64,8192]{2,1,0:T(8,128)(2,1)S(1)} %copy-done) | data formatting | bytes 4194304 | tf_op args[0]
  104.6 29.9 %all_gather.15 = f32[2,64,128]{1,0,2:T(2,128)S(1)} all-gather(f32[2,64,4]{1,0,2:T(2,128)S(1)} %copy.47), channel_id=1, replica_groups=mesh['dp'=32,'head'=16] {'dp'}, dimensions={2}, use_global_device_ids=true | all-gather | bytes 67584 | tf_op jit(solution)/shard_map/all_gather | solution.py:73
  134.8 29.0 %all_gather.16 = f32[2,64,128]{1,0,2:T(2,128)S(1)} all-gather(f32[2,64,4]{1,0,2:T(2,128)S(1)} %copy.50), channel_id=1, replica_groups=mesh['dp'=32,'head'=16] {'dp'}, dimensions={2}, use_global_device_ids=true | all-gather | bytes 67584 | tf_op jit(solution)/shard_map/all_gather | solution.py:74
  164.4 0.8 broadcast_in_dim.118
  165.3 1.5 reshape.150
  166.8 7.1 %bitcast_reduce_fusion = f32[2,64,64]{1,0,2:T(2,128)S(1)} fusion(bf16[2,64,8192]{1,0,2:T(2,128)(2,1)} %copy.46), kind=kLoop, calls=%fused_computation.31 | loop fusion | flops 2088960 | bytes 2129920 | tf_op jit(solution)/shard_map/reduce_sum | solution.py:14
  174.0 22.7 %all-to-all-start.2 = ((bf16[16,2,8192]{2,1,0:T(2,128)(2,1)}), bf16[16,2,8192]{2,1,0:T(2,128)(2,1)S(1)}, u32[]{:S(2)}, u32[]{:S(2)}) async-start(bf16[16,2,8192]{2,1,0:T(2,128)(2,1)} %reshape.150), calls=%async_computation.2 | async-start | bytes 1048576 | tf_op jit(solution)/shard_map/all_to_all | solution.py:87
  196.7 10.5 %fusion.18 = f32[2,64,64]{1,0,2:T(2,128)S(1)} fusion(bf16[2,64,8192]{1,0,2:T(2,128)(2,1)} %copy.46, f32[2,64,64]{1,0,2:T(2,128)S(1)} %broadcast_multiply_fusion.1), kind=kLoop, calls=%fused_computation.33 | loop fusion | flops 4186112 | bytes 2162688 | tf_op jit(solution)/shard_map/reduce_sum | solution.py:15
  207.2 39.8 %fusion.16 = bf16[2,64,8192]{1,0,2:T(2,128)(2,1)} fusion(bf16[2,64,8192]{1,0,2:T(2,128)(2,1)} %copy.46, pred[2,64]{1,0:T(4,128)(4,1)S(1)} %broadcast_compare_fusion, f32[2,64,64]{1,0,2:T(2,128)S(1)} %add_rsqrt_fusion.1, f32[2,64,64]{1,0,2:T(2,128)S(1)} %broadcast_multiply_fusion.1, f32[8192]{0:T(1024)S(1)} %bitcast.179, f32[8192]{0:T(1024)S(1)} %bitcast.178, ...), kind=kLoop, calls=%fused_computation.28 | loop fusion | flops 8388608 | bytes 4391040 | tf_op jit(solution)/shard_map/convert_element_type | solution.py:20
  247.0 7.5 %reshape.146 = bf16[16,2,32768]{2,1,0:T(2,128)(2,1)} reshape(bf16[8192,2,64]{2,1,0:T(2,128)(2,1)} %bitcast.159) | data formatting | bytes 4194304
  254.5 0.8 copy-done.1
  255.3 7.2 %all-to-all-start = ((bf16[16,2,32768]{2,1,0:T(2,128)(2,1)}), bf16[16,2,32768]{2,1,0:T(2,128)(2,1)S(1)}, u32[]{:S(2)}, u32[]{:S(2)}) async-start(bf16[16,2,32768]{2,1,0:T(2,128)(2,1)} %reshape.146), calls=%async_computation | async-start | bytes 4194304 | tf_op jit(solution)/shard_map/all_to_all | solution.py:82
  262.6 59.4 %all-gather = s32[16,64,2]{1,2,0:T(2,128)S(1)} all-gather(s32[1,64,2]{1,2,0:T(2,128)S(1)} %bitcast.181), channel_id=1, replica_groups=mesh['dp'=32,'head'=16] {'head'}, dimensions={0}, use_global_device_ids=true | all-gather | bytes 8704 | tf_op jit(solution)/shard_map/all_gather | solution.py:71
  322.0 3.0 reshape.149
  325.0 1.8 copy.71
  326.9 3.0 reshape.151
  329.9 1.9 copy.74
  331.8 5.0 %reshape.147 = bf16[8192,2,64]{2,1,0:T(2,128)(2,1)} reshape(bf16[16,2,32768]{2,1,0:T(2,128)(2,1)S(1)} %all-to-all-done) | data formatting | bytes 4194304
  336.8 10.6 %copy.53 = bf16[2,16,64,512]{3,2,1,0:T(8,128)(2,1)} copy(bf16[2,16,64,512]{2,0,3,1:T(2,128)(2,1)} %bitcast.158) | data formatting | bytes 4194304 | tf_op jit(solution)/shard_map/all_to_all | solution.py:82
  347.4 52.1 %while.23 = (s32[]{:T(128)}, bf16[2,1024,512]{2,1,0:T(8,128)(2,1)}, bf16[2,1024,512]{2,1,0:T(8,128)(2,1)}, s32[2,1024]{1,0:T(2,128)S(1)}, bf16[2,1024,128]{2,1,0...) while((s32[]{:T(128)}, bf16[2,1024,512]{2,1,0:T(8,128)(2,1)}, ...), condition=%wide.region_9.10_spmd.clone, body=%wide.region_4.9_spmd.clone.sunk | while | flops 1100739072 | bytes 39930744 | solution.py:67
  347.4 1.1 dynamic-slice_bitcast_fusion.2
  348.4 0.8 copy.91
  349.8 0.6 fusion.30
  350.3 1.3 constant_dynamic-slice_fusion.9
  352.0 20.3 %while.24 = (s32[]{:T(128)}, bf16[2,512,512]{2,1,0:T(8,128)(2,1)S(1)}, s32[1024]{0:T(1024)S(1)}, s32[2]{0:T(128)S(1)}, s32[2,512]{1,0:T(2,128)S(1)}, /*index=5*/...) while((s32[]{:T(128)}, ...), condition=%wide.region_8.8_spmd, body=%wide.region_5.7_spmd.sunk | while | flops 1100739072 | bytes 32041108 | solution.py:64
  352.0 0.6 dynamic_slice.48
  353.1 0.5 compare_and_fusion.2
  353.8 1.8 fusion.33
  355.6 2.4 fusion.34
  358.0 3.8 fusion.35
  362.1 0.6 dynamic_slice.48
  364.0 1.8 fusion.33
  365.8 2.4 fusion.34
  368.2 3.8 fusion.35
  372.3 1.0 bitcast_dynamic-update-slice_fusion.2
  373.3 1.1 dynamic-slice_bitcast_fusion.2
  374.4 0.8 copy.91
  375.7 0.6 fusion.30
  376.3 1.3 constant_dynamic-slice_fusion.9
  377.9 20.3 %while.24 = (s32[]{:T(128)}, bf16[2,512,512]{2,1,0:T(8,128)(2,1)S(1)}, s32[1024]{0:T(1024)S(1)}, s32[2]{0:T(128)S(1)}, s32[2,512]{1,0:T(2,128)S(1)}, /*index=5*/...) while((s32[]{:T(128)}, ...), condition=%wide.region_8.8_spmd, body=%wide.region_5.7_spmd.sunk | while | flops 1100739072 | bytes 32041108 | solution.py:64
  377.9 0.6 dynamic_slice.48
  379.8 1.8 fusion.33
  381.6 2.4 fusion.34
  384.0 3.8 fusion.35
  388.1 0.6 dynamic_slice.48
  389.9 1.8 fusion.33
  391.7 2.4 fusion.34
  394.1 3.8 fusion.35
  398.2 1.0 bitcast_dynamic-update-slice_fusion.2
  399.5 3.8 copy.68
  403.3 56.7 %all_to_all.72 = bf16[2,1024,512]{2,0,1:T(2,128)(2,1)S(1)} all-to-all(bf16[2,1024,512]{2,0,1:T(2,128)(2,1)S(1)} %copy.68), channel_id=1, replica_groups=mesh['dp'=32,'head'=16] {'head'}, dimensions={1} | all-to-all | bytes 4194304 | tf_op jit(solution)/shard_map/all_to_all | solution.py:90
  460.0 1.2 copy.69
  461.2 2.3 all_to_all.67
  (73 shorter events, 7.0 us)
Async XLA Ops:
  0.0 97.7 %copy-start = (bf16[2,64,8192]{2,1,0:T(8,128)(2,1)S(1)}, bf16[2,64,8192]{2,1,0:T(8,128)(2,1)}, u32[]{:S(2)}) copy-start(bf16[2,64,8192]{2,1,0:T(8,128)(2,1)} %param.13) | copy-start | bytes 6291460
  0.0 104.6 %copy-start.3 = (f32[2,64,4]{1,2,0:T(4,128)S(1)}, f32[2,64,4]{1,2,0:T(4,128)}, u32[]{:S(2)}) copy-start(f32[2,64,4]{1,2,0:T(4,128)} %param.18) | copy-start | bytes 6148
  0.0 134.8 %copy-start.4 = (f32[2,64,4]{1,2,0:T(4,128)S(1)}, f32[2,64,4]{1,2,0:T(4,128)}, u32[]{:S(2)}) copy-start(f32[2,64,4]{1,2,0:T(4,128)} %param.19) | copy-start | bytes 6148
  0.8 163.2 %copy-start.2 = (bf16[2,64,1024]{2,1,0:T(8,128)(2,1)S(1)}, bf16[2,64,1024]{2,1,0:T(8,128)(2,1)}, u32[]{:S(2)}) copy-start(bf16[2,64,1024]{2,1,0:T(8,128)(2,1)} %param.15) | copy-start | bytes 786436
  70.3 103.6 %all-to-all-start.1 = ((bf16[16,2,8192]{2,1,0:T(2,128)(2,1)}), bf16[16,2,8192]{2,1,0:T(2,128)(2,1)}, u32[]{:S(2)}, u32[]{:S(2)}) async-start(bf16[16,2,8192]{2,1,0:T(2,128)(2,1)} %reshape.148), calls=%async_computation.1 | async-start | bytes 1048576 | tf_op jit(solution)/shard_map/all_to_all | solution.py:84
  174.0 80.6 %all-to-all-start.2 = ((bf16[16,2,8192]{2,1,0:T(2,128)(2,1)}), bf16[16,2,8192]{2,1,0:T(2,128)(2,1)S(1)}, u32[]{:S(2)}, u32[]{:S(2)}) async-start(bf16[16,2,8192]{2,1,0:T(2,128)(2,1)} %reshape.150), calls=%async_computation.2 | async-start | bytes 1048576 | tf_op jit(solution)/shard_map/all_to_all | solution.py:87
  207.2 55.3 %copy-start.5 = (s32[2,64]{1,0:T(2,128)S(1)}, s32[2,64]{1,0:T(2,128)}, u32[]{:S(2)}) copy-start(s32[2,64]{1,0:T(2,128)} %param.16) | copy-start | bytes 1540
  254.5 0.8 copy-start.1
  255.3 76.4 %all-to-all-start = ((bf16[16,2,32768]{2,1,0:T(2,128)(2,1)}), bf16[16,2,32768]{2,1,0:T(2,128)(2,1)S(1)}, u32[]{:S(2)}, u32[]{:S(2)}) async-start(bf16[16,2,32768]{2,1,0:T(2,128)(2,1)} %reshape.146), calls=%async_computation | async-start | bytes 4194304 | tf_op jit(solution)/shard_map/all_to_all | solution.py:82
where the time goes:
time: 469 us; the launch traced here: 464 us
  blocking collectives  236 us (50%)
  local copies, waits for them, and re-layouts  73.7 us (16%)
  other arithmetic  71 us (15%)
  starting transfers between devices  57.3 us (12%)
  matrix products  22.4 us (5%)
    all_gather x1, blocking collectives, on_device(): seg_whole = lax.all_gather(segments, 'head', axis=1, tiled=True)  59.4 us
    all_to_all x1, blocking collectives, on_device(): lax.all_to_all(mixed, 'head', split_axis=1, concat_axis=2, tiled=True)  56.7 us
    convert_element_type x2, other arithmetic, normalize(): return normed.astype(jnp.bfloat16).reshape(packs, rows, width)  40.3 us
    all_gather x1, blocking collectives, on_device(): lax.all_gather(k_scale, 'dp', axis=2, tiled=True)  32.3 us
    unnamed x29, local copies, waits for them, and re-layouts  32.1 us
    all_gather x1, blocking collectives, on_device(): lax.all_gather(q_scale, 'dp', axis=2, tiled=True)  29.9 us
    all_gather x1, blocking collectives, on_device(): lax.all_gather(q_shift, 'dp', axis=2, tiled=True)  29 us
    all_gather x1, blocking collectives, on_device(): lax.all_gather(k_shift, 'dp', axis=2, tiled=True)  28.7 us
  transfers between devices with their start and end apart: 3, of which 0 were waited for; matrix products, arithmetic and copies ran while one was open for 18% of the time, Pallas kernels for 0%

commit v1 on v0

v1 whole, which is shorter than its diff:
```python
import functools
import math

import jax
import jax.numpy as jnp
from jax import lax
from jax.experimental import pallas as pl
from jax.experimental.pallas import tpu as pltpu
from jax.sharding import PartitionSpec as P

KV = 8
GROUP = 8
HD = 128
ROWS = 64
META = 16
ROWS_ALL = 2 * ROWS + META
PARAMS = 384
STRAIGHT = 5
MASKED = -1e30


def pairs(hops, count):
    return [(2 * z + c, 2 * (z + hops) + c) for z in range(count // 2 - hops) for c in (0, 1)]


def normed(x, gain, shift):
    center = x - jnp.mean(x, axis=-1, keepdims=True)
    spread = jnp.mean(center * center, axis=-1, keepdims=True)
    return (center * lax.rsqrt(spread + 1e-05) * gain + shift).astype(jnp.bfloat16)


def attend_kernel(count, q_ref, *refs):
    chunks = [(ref, 0) for ref in refs[: STRAIGHT]]
    chunks += [(refs[STRAIGHT], i * ROWS_ALL) for i in range(count - STRAIGHT)]
    params_ref = refs[STRAIGHT + 1]
    out_ref = refs[-1]
    table = params_ref[...].T

    def pick(image, first, second):
        return jnp.where(image, table[second], table[first])

    metas = [c[at + 2 * ROWS : at + ROWS_ALL, :HD].astype(jnp.float32) for c, at in chunks]
    images = [meta[1:2] > 0.5 for meta in metas]

    span = ROWS * count
    key_seg = jnp.concatenate([meta[0:1, :ROWS] for meta in metas], axis=1)
    key_block = jnp.concatenate([meta[2:3, :ROWS] for meta in metas], axis=1)
    query_seg = jnp.broadcast_to(metas[0][0:1], (HD, HD)).T[:ROWS, 0:1]
    query_block = metas[0][2:3, 0:1]
    key_at = lax.broadcasted_iota(jnp.int32, (ROWS, span), 1)
    query_at = lax.broadcasted_iota(jnp.int32, (ROWS, span), 0)
    past = ((key_at >= ROWS) & (key_block < query_block)) | (key_at <= query_at)
    bias = jnp.where((query_seg == key_seg) & past, 0.0, MASKED)

    for j in range(KV):
        lanes = slice(j * HD, (j + 1) * HD)
        k_normed = []
        for (c, at), image in zip(chunks, images):
            gain = pick(image, slice(256 + j, 257 + j), slice(264 + j, 265 + j))
            shift = pick(image, slice(272 + j, 273 + j), slice(280 + j, 281 + j))
            k_normed.append(normed(c[at : at + ROWS, lanes].astype(jnp.float32), gain, shift))
        keys = jnp.concatenate(k_normed, axis=0)
        values = jnp.concatenate(
            [c[at + ROWS : at + 2 * ROWS, lanes] for c, at in chunks], axis=0
        )
        values = jnp.concatenate([values, jnp.ones_like(values)], axis=1)

        first = GROUP * j
        gains = pick(images[0], slice(first, first + 8), slice(64 + first, 72 + first))
        shifts = pick(images[0], slice(128 + first, 136 + first), slice(192 + first, 200 + first))
        queries = jnp.concatenate(
            [
                normed(
                    q_ref[0, :, (first + h) * HD : (first + h + 1) * HD].astype(jnp.float32),
                    gains[h : h + 1],
                    shifts[h : h + 1],
                )
                for h in range(GROUP)
            ],
            axis=0,
        )
        scores = lax.dot_general(
            queries, keys, (((1,), (1,)), ((), ())), preferred_element_type=jnp.float32
        ) * (HD**-0.5 * math.log2(math.e))
        scores = (scores.reshape(GROUP, ROWS, span) + bias[None]).reshape(GROUP * ROWS, span)
        weights = jnp.exp2(scores - jnp.max(scores, axis=-1, keepdims=True))
        mixed = jnp.dot(weights.astype(jnp.bfloat16), values, preferred_element_type=jnp.float32)
        result = (mixed[:, :HD] * (1.0 / mixed[:, HD:])).astype(out_ref.dtype)
        for h in range(GROUP):
            lane = (first + h) * HD
            out_ref[0, :, lane : lane + HD] = result[h * ROWS : (h + 1) * ROWS]


def attend(pack, queries, straight, crossed, params, earlier):
    count = len(straight) + crossed.shape[0] // ROWS_ALL
    wide = queries.shape[2]
    span = count * ROWS
    in_specs = [pl.BlockSpec((1, ROWS, wide), lambda i: (pack, 0, 0))]
    in_specs += [pl.BlockSpec(x.shape, lambda i: (0, 0)) for x in (*straight, crossed)]
    in_specs += [pl.BlockSpec((HD, PARAMS), lambda i: (0, 0))]
    operands = [queries, *straight, crossed, params]
    aliases = {}
    if earlier is not None:
        aliases = {len(operands): 0}
        operands.append(earlier)
        in_specs.append(pl.BlockSpec(memory_space=pl.ANY))
    return pl.pallas_call(
        functools.partial(attend_kernel, count),
        grid=(1,),
        in_specs=in_specs,
        out_specs=pl.BlockSpec((1, ROWS, wide), lambda i: (pack, 0, 0)),
        out_shape=jax.ShapeDtypeStruct(queries.shape, queries.dtype),
        input_output_aliases=aliases,
        compiler_params=pltpu.CompilerParams(vmem_limit_bytes=40 * 1024 * 1024),
        cost_estimate=pl.CostEstimate(
            flops=KV * GROUP * ROWS * span * HD * 6,
            bytes_accessed=2 * ROWS * wide * 2 + count * ROWS_ALL * KV * HD * 2,
            transcendentals=KV * GROUP * ROWS * span,
        ),
        name="attend",
    )(*operands)


def gather_params(q_scale, q_shift, k_scale, k_shift):
    copies = lax.axis_size("dp")
    width = q_scale.shape[2]
    mine = jnp.concatenate(
        [x.reshape(-1, width) for x in (q_scale, q_shift, k_scale, k_shift)], axis=0
    ).T
    mine = jnp.pad(mine, ((0, 0), (0, PARAMS - mine.shape[1])))
    sent = jnp.broadcast_to(mine[None], (copies, *mine.shape))
    whole = lax.all_to_all(sent, "dp", split_axis=0, concat_axis=0, tiled=True)
    return whole.reshape(copies * width, PARAMS)


def on_device(queries, keys, values, segments, modality, q_scale, q_shift, k_scale, k_shift):
    count = lax.axis_size("head")
    packs = queries.shape[0]
    place = lax.axis_index("head")
    odd = place % 2 == 1
    swap = [(i, i ^ 1) for i in range(count)]

    def send(x, hops):
        return lax.ppermute(x, "head", pairs(hops, count))

    def cross(x):
        return lax.ppermute(x, "head", swap)

    marks = jnp.concatenate([segments + 1, jnp.zeros_like(segments)], axis=1)
    marks = jnp.tile(marks, (1, KV))
    kinds = jnp.broadcast_to(modality[:, :1], marks.shape)
    places = jnp.broadcast_to(place.astype(marks.dtype), marks.shape)
    meta = jnp.stack([marks, kinds, places], axis=1).astype(keys.dtype)
    meta = jnp.pad(meta, ((0, 0), (0, META - 3), (0, 0)))
    own = [jnp.concatenate([keys[p], values[p], meta[p]], axis=0) for p in range(packs)]

    params = gather_params(q_scale, q_shift, k_scale, k_shift)
    first = [send(x, 1) for x in own]
    second = [send(x, 1) for x in first]
    second[-1], params = lax.optimization_barrier((second[-1], params))
    third = [send(x, 1) for x in second]
    fourth = [send(x, 1) for x in third]
    out = None
    crossed = []
    for p in range(packs):
        lacking = jnp.where(odd, fourth[p], own[p])
        crossed.append(cross(jnp.concatenate([first[p], second[p], third[p], lacking], axis=0)))
    for p in range(packs):
        straight = [own[p], first[p], second[p], third[p], fourth[p]]
        out = attend(p, queries, straight, crossed[p], params, out)
    return out


def solution(mesh):
    rows = P("dp", "head", None)
    marks = P("dp", "head")
    norms = P(None, None, "dp")
    placed = (rows, rows, rows, marks, marks, norms, norms, norms, norms)
    return jax.shard_map(
        on_device, mesh=mesh, in_specs=placed, out_specs=rows, check_vma=False
    )
```

time: 469 us -> 83.5 us (0.18)
  the two profiles are of different devices: /device:TPU:1 before, /device:TPU:195 now
where the time goes in v1:
time: 83.5 us; the launch traced here: 83 us
  starting transfers between devices  50.2 us (60%)
  Pallas kernels  14.1 us (17%)
  waiting for transfers between devices  13.9 us (17%)
  local copies, waits for them, and re-layouts  2.47 us (3%)
  other arithmetic  2.03 us (2%)
    ppermute x8, starting transfers between devices, send(): return lax.ppermute(x, 'head', pairs(hops, count))  27.9 us
    pallas_call x2, Pallas kernels, attend(): pl.pallas_call(functools.partial(attend_kernel, count), grid=(1,), in_spe...  14.1 us
    ppermute x2, starting transfers between devices, cross(): return lax.ppermute(x, 'head', swap)  12.7 us
    ppermute x8, waiting for transfers between devices, send(): return lax.ppermute(x, 'head', pairs(hops, count))  10.7 us
    all_to_all x1, starting transfers between devices, gather_params(): whole = lax.all_to_all(sent, 'dp', split_axis=0, concat_axis=0, tiled=True)  9.69 us
    all_to_all x1, waiting for transfers between devices, gather_params(): whole = lax.all_to_all(sent, 'dp', split_axis=0, concat_axis=0, tiled=True)  3.22 us
  transfers between devices with their start and end apart: 11, of which 5 were waited for; matrix products, arithmetic and copies ran while one was open for 2% of the time, Pallas kernels for 8%

profile of v1, /device:TPU:195, one launch (start us, length us, event | category | flops | bytes accessed | tf_op | source)
XLA Modules:
  0.0 83.0 jit_solution(10162259909198744747)
XLA Ops:
  0.0 0.0 copy-start.1
  0.0 0.0 copy-start.2
  0.0 0.0 copy-start.3
  0.0 0.0 copy-start.4
  0.0 0.7 broadcast_add_fusion
  0.8 0.8 fusion.2
  1.6 0.1 pad.31.clone
  1.6 0.1 stack_broadcast_in_dim.8
  1.7 0.1 maximum_maximum_fusion
  1.8 1.1 %slice_bitcast_fusion = (bf16[64,1024]{1,0:T(8,128)(2,1)S(1)}, bf16[64,1024]{1,0:T(8,128)(2,1)S(1)}, bf16[64,1024]{1,0:T(8,128)(2,1)S(1)}, bf16[64,1024]{1,0:T(8,128)(2,1)S(1)}) fusion(bf16[2,64,1024]{2,1,0:T(8,128)(2,1)} %param.11, bf16[2,64,1024]{2,1,0:T(8,128)(2,1)} %param.10), kind=kLoop, calls=%fused_computation.6 | loop fusion | bytes 1048576 | tf_op jit(solution)/shard_map/squeeze | solution.py:155
  3.0 5.2 %collective-permute-start.5 = (bf16[144,1024]{1,0:T(8,128)(2,1)S(1)}, bf16[144,1024]{1,0:T(8,128)(2,1)S(1)}, u32[]{:S(2)}, u32[]{:S(2)}) collective-permute-start(bf16[144,1024]{1,0:T(8,128)(2,1)S(1)} %pad_maximum_fusion.3.refs_0_), channel_id=1, source_target_pairs={{0,2},{1,3},{2,4},{3,5},{4,6},{5,7},{6,8},{7,9},{8,10},{9,11},{10,... | collective-permute-start | bytes 884744 | tf_op jit(solution)/shard_map/ppermute | solution.py:144
  8.2 3.1 %collective-permute-start = (bf16[144,1024]{1,0:T(8,128)(2,1)S(1)}, bf16[144,1024]{1,0:T(8,128)(2,1)S(1)}, u32[]{:S(2)}, u32[]{:S(2)}) collective-permute-start(bf16[144,1024]{1,0:T(8,128)(2,1)S(1)} %pad_maximum_fusion.2.refs_0_), channel_id=1, source_target_pairs={{0,2},{1,3},{2,4},{3,5},{4,6},{5,7},{6,8},{7,9},{8,10},{9,11},{10,... | collective-permute-start | bytes 884744 | tf_op jit(solution)/shard_map/ppermute | solution.py:144
  11.3 2.5 %collective-permute-done.5.refs_1_ = bf16[144,1024]{1,0:T(8,128)(2,1)S(1)} collective-permute-done((bf16[144,1024]{1,0:T(8,128)(2,1)S(1)}, bf16[144,1024]{1,0:T(8,128)(2,1)S(1)}, u32[]{:S(2)}, u32[]{:S(2)}) %collective-permute-start.5) | collective-permute-done | bytes 294944 | tf_op jit(solution)/shard_map/ppermute | solution.py:144
  13.9 5.3 %collective-permute-start.6 = (bf16[144,1024]{1,0:T(8,128)(2,1)S(1)}, bf16[144,1024]{1,0:T(8,128)(2,1)S(1)}, u32[]{:S(2)}, u32[]{:S(2)}) collective-permute-start(bf16[144,1024]{1,0:T(8,128)(2,1)S(1)} %collective-permute-done.5.refs_1_), channel_id=1, source_target_pairs={{0,2},{1,3},{2,4},{3,5},{4,6},{5,7},{6,8},{7,9},{8,10},{9,11},{10,... | collective-permute-start | bytes 884744 | tf_op jit(solution)/shard_map/ppermute | solution.py:144
  19.2 0.0 copy-done.1
  19.2 0.1 reshape.26
  19.3 0.0 copy-done.2
  19.3 0.1 reshape.27
  19.4 0.0 copy-done.3
  19.4 0.1 reshape.28
  19.5 0.0 copy-done.4
  19.5 0.1 reshape.29
  19.5 0.1 maximum_bitcast_fusion
  19.6 0.7 broadcast_in_dim.2
  20.3 9.7 %all-to-all-start = ((f32[32,4,384]{2,1,0:T(4,128)}), f32[32,4,384]{2,1,0:T(4,128)S(1)}, u32[]{:S(2)}, u32[]{:S(2)}) async-start(f32[32,4,384]{2,1,0:T(4,128)} %broadcast_in_dim.2), calls=%async_computation | async-start | bytes 393216 | tf_op jit(solution)/shard_map/all_to_all | solution.py:132
  30.0 0.0 collective-permute-done.refs_1_
  30.0 1.9 %collective-permute-start.1 = (bf16[144,1024]{1,0:T(8,128)(2,1)S(1)}, bf16[144,1024]{1,0:T(8,128)(2,1)S(1)}, u32[]{:S(2)}, u32[]{:S(2)}) collective-permute-start(bf16[144,1024]{1,0:T(8,128)(2,1)S(1)} %collective-permute-done.refs_1_), channel_id=1, source_target_pairs={{0,2},{1,3},{2,4},{3,5},{4,6},{5,7},{6,8},{7,9},{8,10},{9,11},{10,... | collective-permute-start | bytes 884744 | tf_op jit(solution)/shard_map/ppermute | solution.py:144
  32.0 0.0 collective-permute-done.6.refs_2_
  32.0 3.1 %collective-permute-start.7 = (bf16[144,1024]{1,0:T(8,128)(2,1)S(1)}, bf16[144,1024]{1,0:T(8,128)(2,1)S(1)}, u32[]{:S(2)}, u32[]{:S(2)}) collective-permute-start(bf16[144,1024]{1,0:T(8,128)(2,1)S(1)} %collective-permute-done.6.refs_2_), channel_id=1, source_target_pairs={{0,2},{1,3},{2,4},{3,5},{4,6},{5,7},{6,8},{7,9},{8,10},{9,11},{10,... | collective-permute-start | bytes 884744 | tf_op jit(solution)/shard_map/ppermute | solution.py:144
  35.1 3.2 %all-to-all-done = f32[32,4,384]{2,1,0:T(4,128)S(1)} async-done(((f32[32,4,384]{2,1,0:T(4,128)}), f32[32,4,384]{2,1,0:T(4,128)S(1)}, u32[]{:S(2)}, u32[]{:S(2)}) %all-to-all-start) | async-done | bytes 196640 | tf_op jit(solution)/shard_map/all_to_all | solution.py:132
  38.3 0.1 reshape.30.refs_6_
  38.4 0.0 collective-permute-done.1.refs_2_
  38.4 2.6 %collective-permute-start.2 = (bf16[144,1024]{1,0:T(8,128)(2,1)S(1)}, bf16[144,1024]{1,0:T(8,128)(2,1)S(1)}, u32[]{:S(2)}, u32[]{:S(2)}) collective-permute-start(bf16[144,1024]{1,0:T(8,128)(2,1)S(1)} %collective-permute-done.1.refs_2_), channel_id=1, source_target_pairs={{0,2},{1,3},{2,4},{3,5},{4,6},{5,7},{6,8},{7,9},{8,10},{9,11},{10,... | collective-permute-start | bytes 884744 | tf_op jit(solution)/shard_map/ppermute | solution.py:144
  40.9 2.3 %collective-permute-done.7.refs_3_ = bf16[144,1024]{1,0:T(8,128)(2,1)S(1)} collective-permute-done((bf16[144,1024]{1,0:T(8,128)(2,1)S(1)}, bf16[144,1024]{1,0:T(8,128)(2,1)S(1)}, u32[]{:S(2)}, u32[]{:S(2)}) %collective-permute-start.7) | collective-permute-done | bytes 294944 | tf_op jit(solution)/shard_map/ppermute | solution.py:144
  43.2 3.1 %collective-permute-start.8 = (bf16[144,1024]{1,0:T(8,128)(2,1)S(1)}, bf16[144,1024]{1,0:T(8,128)(2,1)S(1)}, u32[]{:S(2)}, u32[]{:S(2)}) collective-permute-start(bf16[144,1024]{1,0:T(8,128)(2,1)S(1)} %collective-permute-done.7.refs_3_), channel_id=1, source_target_pairs={{0,2},{1,3},{2,4},{3,5},{4,6},{5,7},{6,8},{7,9},{8,10},{9,11},{10,... | collective-permute-start | bytes 884744 | tf_op jit(solution)/shard_map/ppermute | solution.py:144
  46.4 3.2 %collective-permute-done.2.refs_3_ = bf16[144,1024]{1,0:T(8,128)(2,1)S(1)} collective-permute-done((bf16[144,1024]{1,0:T(8,128)(2,1)S(1)}, bf16[144,1024]{1,0:T(8,128)(2,1)S(1)}, u32[]{:S(2)}, u32[]{:S(2)}) %collective-permute-start.2) | collective-permute-done | bytes 294944 | tf_op jit(solution)/shard_map/ppermute | solution.py:144
  49.5 3.6 %collective-permute-start.3 = (bf16[144,1024]{1,0:T(8,128)(2,1)S(1)}, bf16[144,1024]{1,0:T(8,128)(2,1)S(1)}, u32[]{:S(2)}, u32[]{:S(2)}) collective-permute-start(bf16[144,1024]{1,0:T(8,128)(2,1)S(1)} %collective-permute-done.2.refs_3_), channel_id=1, source_target_pairs={{0,2},{1,3},{2,4},{3,5},{4,6},{5,7},{6,8},{7,9},{8,10},{9,11},{10,... | collective-permute-start | bytes 884744 | tf_op jit(solution)/shard_map/ppermute | solution.py:144
  53.1 2.7 %collective-permute-done.8.refs_4_ = bf16[144,1024]{1,0:T(8,128)(2,1)S(1)} collective-permute-done((bf16[144,1024]{1,0:T(8,128)(2,1)S(1)}, bf16[144,1024]{1,0:T(8,128)(2,1)S(1)}, u32[]{:S(2)}, u32[]{:S(2)}) %collective-permute-start.8) | collective-permute-done | bytes 294944 | tf_op jit(solution)/shard_map/ppermute | solution.py:144
  55.9 0.1 broadcast_select_fusion
  56.0 0.1 pad_maximum_fusion.1
  56.0 0.0 copy-start
  56.1 9.7 %collective-permute-start.9 = (bf16[576,1024]{1,0:T(8,128)(2,1)S(1)}, bf16[576,1024]{1,0:T(8,128)(2,1)S(1)}, u32[]{:S(2)}, u32[]{:S(2)}) collective-permute-start(bf16[576,1024]{1,0:T(8,128)(2,1)S(1)} %pad_maximum_fusion.1), channel_id=1, source_target_pairs={{0,1},{1,0},{2,3},{3,2},{4,5},{5,4},{6,7},{7,6},{8,9},{9,8},{10,11... | collective-permute-start | bytes 3538952 | tf_op jit(solution)/shard_map/ppermute | solution.py:147
  65.7 0.0 collective-permute-done.3.refs_4_
  65.7 0.1 broadcast_select_fusion.1
  65.8 0.1 pad_maximum_fusion
  65.9 3.0 %collective-permute-start.4 = (bf16[576,1024]{1,0:T(8,128)(2,1)S(1)}, bf16[576,1024]{1,0:T(8,128)(2,1)S(1)}, u32[]{:S(2)}, u32[]{:S(2)}) collective-permute-start(bf16[576,1024]{1,0:T(8,128)(2,1)S(1)} %pad_maximum_fusion), channel_id=1, source_target_pairs={{0,1},{1,0},{2,3},{3,2},{4,5},{5,4},{6,7},{7,6},{8,9},{9,8},{10,11... | collective-permute-start | bytes 3538952 | tf_op jit(solution)/shard_map/ppermute | solution.py:147
  68.9 0.0 collective-permute-done.9.refs_5_
  68.9 0.0 copy-done
  69.0 7.0 %attend.2.refs_7_ = bf16[2,64,8192]{2,1,0:T(8,128)(2,1)} custom-call(bf16[2,64,8192]{2,1,0:T(8,128)(2,1)S(1)} %copy-done, bf16[144,1024]{1,0:T(8,128)(2,1)S(1)} %pad_maximum_fusion.3.refs_0_, bf16[144,1024]{1,0:T(8,128)(2,1)S(1)} %collective-permute-done.5.refs_1_, bf16[144,1024]{1,0:T(8,128)(2,1)S(1)} %collective-permute-done.6.refs_2_, ...), custom_call_target="tpu_custom_call" | custom-call | flops 1811939328 | bytes 4751360 | tf_op jit(solution)/shard_map/attend/pallas_call | solution.py:107
  76.0 0.0 collective-permute-done.4.refs_5_
  76.0 7.0 %attend.3 = bf16[2,64,8192]{2,1,0:T(8,128)(2,1)} custom-call(bf16[2,64,8192]{2,1,0:T(8,128)(2,1)S(1)} %copy-done, bf16[144,1024]{1,0:T(8,128)(2,1)S(1)} %pad_maximum_fusion.2.refs_0_, bf16[144,1024]{1,0:T(8,128)(2,1)S(1)} %collective-permute-done.refs_1_, bf16[144,1024]{1,0:T(8,128)(2,1)S(1)} %collective-permute-done.1.refs_2_, ...), custom_call_target="tpu_custom_call", output_to_operand_aliasing={{}: (8, {})} | custom-call | flops 1811939328 | bytes 4751360 | tf_op jit(solution)/shard_map/attend/pallas_call | solution.py:107
  (11 shorter events, 0.1 us)
Async XLA Ops:
  0.0 19.2 %copy-start.1 = (f32[2,64,4]{1,2,0:T(4,128)S(1)}, f32[2,64,4]{1,2,0:T(4,128)}, u32[]{:S(2)}) copy-start(f32[2,64,4]{1,2,0:T(4,128)} %param.14) | copy-start | bytes 6148
  0.0 19.3 %copy-start.2 = (f32[2,64,4]{1,2,0:T(4,128)S(1)}, f32[2,64,4]{1,2,0:T(4,128)}, u32[]{:S(2)}) copy-start(f32[2,64,4]{1,2,0:T(4,128)} %param.15) | copy-start | bytes 6148
  0.0 19.4 %copy-start.3 = (f32[2,8,4]{1,2,0:T(4,128)S(1)}, f32[2,8,4]{1,2,0:T(4,128)}, u32[]{:S(2)}) copy-start(f32[2,8,4]{1,2,0:T(4,128)} %param.16) | copy-start | bytes 772
  0.0 19.4 %copy-start.4 = (f32[2,8,4]{1,2,0:T(4,128)S(1)}, f32[2,8,4]{1,2,0:T(4,128)}, u32[]{:S(2)}) copy-start(f32[2,8,4]{1,2,0:T(4,128)} %param.17) | copy-start | bytes 772
  3.0 10.9 %collective-permute-start.5 = (bf16[144,1024]{1,0:T(8,128)(2,1)S(1)}, bf16[144,1024]{1,0:T(8,128)(2,1)S(1)}, u32[]{:S(2)}, u32[]{:S(2)}) collective-permute-start(bf16[144,1024]{1,0:T(8,128)(2,1)S(1)} %pad_maximum_fusion.3.refs_0_), channel_id=1, source_target_pairs={{0,2},{1,3},{2,4},{3,5},{4,6},{5,7},{6,8},{7,9},{8,10},{9,11},{10,... | collective-permute-start | bytes 884744 | tf_op jit(solution)/shard_map/ppermute | solution.py:144
  8.2 21.8 %collective-permute-start = (bf16[144,1024]{1,0:T(8,128)(2,1)S(1)}, bf16[144,1024]{1,0:T(8,128)(2,1)S(1)}, u32[]{:S(2)}, u32[]{:S(2)}) collective-permute-start(bf16[144,1024]{1,0:T(8,128)(2,1)S(1)} %pad_maximum_fusion.2.refs_0_), channel_id=1, source_target_pairs={{0,2},{1,3},{2,4},{3,5},{4,6},{5,7},{6,8},{7,9},{8,10},{9,11},{10,... | collective-permute-start | bytes 884744 | tf_op jit(solution)/shard_map/ppermute | solution.py:144
  13.9 18.1 %collective-permute-start.6 = (bf16[144,1024]{1,0:T(8,128)(2,1)S(1)}, bf16[144,1024]{1,0:T(8,128)(2,1)S(1)}, u32[]{:S(2)}, u32[]{:S(2)}) collective-permute-start(bf16[144,1024]{1,0:T(8,128)(2,1)S(1)} %collective-permute-done.5.refs_1_), channel_id=1, source_target_pairs={{0,2},{1,3},{2,4},{3,5},{4,6},{5,7},{6,8},{7,9},{8,10},{9,11},{10,... | collective-permute-start | bytes 884744 | tf_op jit(solution)/shard_map/ppermute | solution.py:144
  20.3 17.9 %all-to-all-start = ((f32[32,4,384]{2,1,0:T(4,128)}), f32[32,4,384]{2,1,0:T(4,128)S(1)}, u32[]{:S(2)}, u32[]{:S(2)}) async-start(f32[32,4,384]{2,1,0:T(4,128)} %broadcast_in_dim.2), calls=%async_computation | async-start | bytes 393216 | tf_op jit(solution)/shard_map/all_to_all | solution.py:132
  30.0 8.3 %collective-permute-start.1 = (bf16[144,1024]{1,0:T(8,128)(2,1)S(1)}, bf16[144,1024]{1,0:T(8,128)(2,1)S(1)}, u32[]{:S(2)}, u32[]{:S(2)}) collective-permute-start(bf16[144,1024]{1,0:T(8,128)(2,1)S(1)} %collective-permute-done.refs_1_), channel_id=1, source_target_pairs={{0,2},{1,3},{2,4},{3,5},{4,6},{5,7},{6,8},{7,9},{8,10},{9,11},{10,... | collective-permute-start | bytes 884744 | tf_op jit(solution)/shard_map/ppermute | solution.py:144
  32.0 11.2 %collective-permute-start.7 = (bf16[144,1024]{1,0:T(8,128)(2,1)S(1)}, bf16[144,1024]{1,0:T(8,128)(2,1)S(1)}, u32[]{:S(2)}, u32[]{:S(2)}) collective-permute-start(bf16[144,1024]{1,0:T(8,128)(2,1)S(1)} %collective-permute-done.6.refs_2_), channel_id=1, source_target_pairs={{0,2},{1,3},{2,4},{3,5},{4,6},{5,7},{6,8},{7,9},{8,10},{9,11},{10,... | collective-permute-start | bytes 884744 | tf_op jit(solution)/shard_map/ppermute | solution.py:144
  38.4 11.2 %collective-permute-start.2 = (bf16[144,1024]{1,0:T(8,128)(2,1)S(1)}, bf16[144,1024]{1,0:T(8,128)(2,1)S(1)}, u32[]{:S(2)}, u32[]{:S(2)}) collective-permute-start(bf16[144,1024]{1,0:T(8,128)(2,1)S(1)} %collective-permute-done.1.refs_2_), channel_id=1, source_target_pairs={{0,2},{1,3},{2,4},{3,5},{4,6},{5,7},{6,8},{7,9},{8,10},{9,11},{10,... | collective-permute-start | bytes 884744 | tf_op jit(solution)/shard_map/ppermute | solution.py:144
  43.2 12.6 %collective-permute-start.8 = (bf16[144,1024]{1,0:T(8,128)(2,1)S(1)}, bf16[144,1024]{1,0:T(8,128)(2,1)S(1)}, u32[]{:S(2)}, u32[]{:S(2)}) collective-permute-start(bf16[144,1024]{1,0:T(8,128)(2,1)S(1)} %collective-permute-done.7.refs_3_), channel_id=1, source_target_pairs={{0,2},{1,3},{2,4},{3,5},{4,6},{5,7},{6,8},{7,9},{8,10},{9,11},{10,... | collective-permute-start | bytes 884744 | tf_op jit(solution)/shard_map/ppermute | solution.py:144
  49.5 16.2 %collective-permute-start.3 = (bf16[144,1024]{1,0:T(8,128)(2,1)S(1)}, bf16[144,1024]{1,0:T(8,128)(2,1)S(1)}, u32[]{:S(2)}, u32[]{:S(2)}) collective-permute-start(bf16[144,1024]{1,0:T(8,128)(2,1)S(1)} %collective-permute-done.2.refs_3_), channel_id=1, source_target_pairs={{0,2},{1,3},{2,4},{3,5},{4,6},{5,7},{6,8},{7,9},{8,10},{9,11},{10,... | collective-permute-start | bytes 884744 | tf_op jit(solution)/shard_map/ppermute | solution.py:144
  56.0 12.9 %copy-start = (bf16[2,64,8192]{2,1,0:T(8,128)(2,1)S(1)}, bf16[2,64,8192]{2,1,0:T(8,128)(2,1)}, u32[]{:S(2)}) copy-start(bf16[2,64,8192]{2,1,0:T(8,128)(2,1)} %q_ref.3) | copy-start | bytes 6291460
  56.1 12.9 %collective-permute-start.9 = (bf16[576,1024]{1,0:T(8,128)(2,1)S(1)}, bf16[576,1024]{1,0:T(8,128)(2,1)S(1)}, u32[]{:S(2)}, u32[]{:S(2)}) collective-permute-start(bf16[576,1024]{1,0:T(8,128)(2,1)S(1)} %pad_maximum_fusion.1), channel_id=1, source_target_pairs={{0,1},{1,0},{2,3},{3,2},{4,5},{5,4},{6,7},{7,6},{8,9},{9,8},{10,11... | collective-permute-start | bytes 3538952 | tf_op jit(solution)/shard_map/ppermute | solution.py:147
  65.9 10.1 %collective-permute-start.4 = (bf16[576,1024]{1,0:T(8,128)(2,1)S(1)}, bf16[576,1024]{1,0:T(8,128)(2,1)S(1)}, u32[]{:S(2)}, u32[]{:S(2)}) collective-permute-start(bf16[576,1024]{1,0:T(8,128)(2,1)S(1)} %pad_maximum_fusion), channel_id=1, source_target_pairs={{0,1},{1,0},{2,3},{3,2},{4,5},{5,4},{6,7},{7,6},{8,9},{9,8},{10,11... | collective-permute-start | bytes 3538952 | tf_op jit(solution)/shard_map/ppermute | solution.py:147

commit v2 on v1

v2 whole, which is shorter than its diff:
```python
import functools
import math

import jax
import jax.numpy as jnp
from jax import lax
from jax.experimental import pallas as pl
from jax.experimental.pallas import tpu as pltpu
from jax.sharding import PartitionSpec as P

KV = 8
GROUP = 8
HD = 128
ROWS = 64
META = 16
MARKS = 3
MARKED_ROWS = 2 * ROWS + META
PARAMS = 384
WINDOW = 9
MASKED = -1e30


def pairs(chips, hops, count):
    ring = count // 2
    return [(2 * (z % ring) + c, 2 * ((z + hops) % ring) + c) for z in chips for c in (0, 1)]


def normed(x, gain, shift):
    center = x - jnp.mean(x, axis=-1, keepdims=True)
    spread = jnp.mean(center * center, axis=-1, keepdims=True)
    return (center * lax.rsqrt(spread + 1e-05) * gain + shift).astype(jnp.bfloat16)


def attend_kernel(pack, blocks, q_ref, *refs):
    meta_refs = refs[:WINDOW]
    chunks = [(refs[WINDOW + i], at) for i, at in blocks]
    params_ref = refs[WINDOW + 1 + blocks[-1][0]]
    out_ref = refs[-1]
    table = params_ref[...].T

    def pick(image, first, second):
        return jnp.where(image, table[second], table[first])

    marks = slice(MARKS * pack, MARKS * (pack + 1))
    metas = [ref[...].astype(jnp.float32)[marks] for ref in meta_refs]
    images = [meta[1:2] > 0.5 for meta in metas]

    span = ROWS * WINDOW
    key_seg = jnp.concatenate([meta[0:1, :ROWS] for meta in metas], axis=1)
    key_block = jnp.concatenate([meta[2:3, :ROWS] for meta in metas], axis=1)
    query_seg = jnp.broadcast_to(metas[0][0:1], (HD, HD)).T[:ROWS, 0:1]
    query_block = metas[0][2:3, 0:1]
    key_at = lax.broadcasted_iota(jnp.int32, (ROWS, span), 1)
    query_at = lax.broadcasted_iota(jnp.int32, (ROWS, span), 0)
    past = ((key_at >= ROWS) & (key_block < query_block)) | (key_at <= query_at)
    bias = jnp.where((query_seg == key_seg) & past, 0.0, MASKED)

    for j in range(KV):
        lanes = slice(j * HD, (j + 1) * HD)
        k_normed = []
        for (ref, at), image in zip(chunks, images):
            gain = pick(image, slice(256 + j, 257 + j), slice(264 + j, 265 + j))
            shift = pick(image, slice(272 + j, 273 + j), slice(280 + j, 281 + j))
            k_normed.append(normed(ref[at : at + ROWS, lanes].astype(jnp.float32), gain, shift))
        keys = jnp.concatenate(k_normed, axis=0)
        values = jnp.concatenate(
            [ref[at + ROWS : at + 2 * ROWS, lanes] for ref, at in chunks], axis=0
        )
        values = jnp.concatenate([values, jnp.ones_like(values)], axis=1)

        first = GROUP * j
        gains = pick(images[0], slice(first, first + 8), slice(64 + first, 72 + first))
        shifts = pick(images[0], slice(128 + first, 136 + first), slice(192 + first, 200 + first))
        queries = jnp.concatenate(
            [
                normed(
                    q_ref[:, (first + h) * HD : (first + h + 1) * HD].astype(jnp.float32),
                    gains[h : h + 1],
                    shifts[h : h + 1],
                )
                for h in range(GROUP)
            ],
            axis=0,
        )
        scores = lax.dot_general(
            queries, keys, (((1,), (1,)), ((), ())), preferred_element_type=jnp.float32
        ) * (HD**-0.5 * math.log2(math.e))
        scores = (scores.reshape(GROUP, ROWS, span) + bias[None]).reshape(GROUP * ROWS, span)
        weights = jnp.exp2(scores - jnp.max(scores, axis=-1, keepdims=True))
        mixed = jnp.dot(weights.astype(jnp.bfloat16), values, preferred_element_type=jnp.float32)
        result = (mixed[:, :HD] * (1.0 / mixed[:, HD:])).astype(out_ref.dtype)
        for h in range(GROUP):
            lane = (first + h) * HD
            out_ref[:, lane : lane + HD] = result[h * ROWS : (h + 1) * ROWS]


def attend(pack, queries, chunks, marked, params, earlier):
    wide = queries.shape[2]
    row_spec = pl.BlockSpec((None, ROWS, wide), lambda i: (pack, 0, 0))
    in_specs, operands = [row_spec], [queries]
    for x in marked:
        for at in range(2 * ROWS, x.shape[0], MARKED_ROWS):
            in_specs.append(pl.BlockSpec((META, HD), lambda i, at=at // META: (at, 0)))
            operands.append(x)
    blocks = []
    for n, x in enumerate(chunks):
        blocks += [(n, at) for at in range(0, x.shape[0], 2 * ROWS if pack == 0 else MARKED_ROWS)]
        in_specs.append(pl.BlockSpec(x.shape, lambda i: (0, 0)))
        operands.append(x)
    in_specs.append(pl.BlockSpec((HD, PARAMS), lambda i: (0, 0)))
    operands.append(params)
    aliases = {}
    if earlier is not None:
        aliases = {len(operands): 0}
        operands.append(earlier)
        in_specs.append(pl.BlockSpec(memory_space=pl.ANY))
    span = WINDOW * ROWS
    return pl.pallas_call(
        functools.partial(attend_kernel, pack, tuple(blocks)),
        grid=(1,),
        in_specs=in_specs,
        out_specs=row_spec,
        out_shape=jax.ShapeDtypeStruct(queries.shape, queries.dtype),
        input_output_aliases=aliases,
        compiler_params=pltpu.CompilerParams(vmem_limit_bytes=40 * 1024 * 1024),
        cost_estimate=pl.CostEstimate(
            flops=KV * GROUP * ROWS * span * HD * 6,
            bytes_accessed=2 * ROWS * wide * 2 + span * KV * HD * 4,
            transcendentals=KV * GROUP * ROWS * span,
        ),
        name="attend",
    )(*operands)


def whole_block(shape):
    return pl.BlockSpec(shape, lambda i: (0,) * len(shape))


def collect_kernel(place_ref, keys_ref, values_ref, segments_ref, modality_ref, *outs):
    both_ref, a_ref, b_ref = outs
    wide = keys_ref.shape[2]
    row = lax.broadcasted_iota(jnp.int32, (META, wide), 0)
    marks = jnp.zeros((META, wide), jnp.int32)
    for p in range(2):
        documents = segments_ref[p : p + 1, :] + 1
        documents = jnp.concatenate([documents, jnp.zeros_like(documents)], axis=1)
        documents = jnp.concatenate([documents] * KV, axis=1)
        kind = jnp.broadcast_to(modality_ref[p : p + 1, 0:1], (1, wide))
        marks = jnp.where(row == MARKS * p, documents, marks)
        marks = jnp.where(row == MARKS * p + 1, kind, marks)
        marks = jnp.where(row == MARKS * p + 2, place_ref[0], marks)
    marks = marks.astype(jnp.float32).astype(both_ref.dtype)
    for p, ref in enumerate((a_ref, b_ref)):
        for at, source in ((0, keys_ref), (ROWS, values_ref)):
            rows = source[p]
            ref[at : at + ROWS, :] = rows
            both_ref[2 * ROWS * p + at : 2 * ROWS * p + at + ROWS, :] = rows
    b_ref[2 * ROWS :, :] = marks
    both_ref[4 * ROWS :, :] = marks


def collect(keys, values, segments, modality, place):
    wide = keys.shape[2]
    shapes = [(4 * ROWS + META, wide), (2 * ROWS, wide), (MARKED_ROWS, wide)]
    return pl.pallas_call(
        collect_kernel,
        grid=(1,),
        in_specs=[pl.BlockSpec(memory_space=pltpu.SMEM)]
        + [whole_block(x.shape) for x in (keys, values, segments, modality)],
        out_specs=[whole_block(shape) for shape in shapes],
        out_shape=[jax.ShapeDtypeStruct(shape, keys.dtype) for shape in shapes],
        compiler_params=pltpu.CompilerParams(vmem_limit_bytes=60 * 1024 * 1024),
        name="collect",
    )(place.astype(jnp.int32).reshape(1), keys, values, segments, modality)


def spread_kernel(*refs):
    out_ref = refs[-1]
    _, width, lanes = out_ref.shape
    parts = [ref[m] for ref in refs[:-1] for m in range(ref.shape[0])]
    filled = sum(part.shape[1] for part in parts)
    parts.append(jnp.zeros((width, lanes - filled), out_ref.dtype))
    out_ref[...] = jnp.broadcast_to(jnp.concatenate(parts, axis=1)[None], out_ref.shape)


def gather_params(*norms):
    copies = lax.axis_size("dp")
    norms = [x.transpose(0, 2, 1) for x in norms]
    width = norms[0].shape[1]
    shape = (copies, width, PARAMS)
    sent = pl.pallas_call(
        spread_kernel,
        grid=(1,),
        in_specs=[whole_block(x.shape) for x in norms],
        out_specs=whole_block(shape),
        out_shape=jax.ShapeDtypeStruct(shape, norms[0].dtype),
        compiler_params=pltpu.CompilerParams(vmem_limit_bytes=60 * 1024 * 1024),
        name="spread",
    )(*norms)
    whole = lax.all_to_all(sent, "dp", split_axis=0, concat_axis=0, tiled=True)
    return whole.reshape(copies * width, PARAMS)


def on_device(queries, keys, values, segments, modality, q_scale, q_shift, k_scale, k_shift):
    count = lax.axis_size("head")
    place = lax.axis_index("head")
    odd = place % 2 == 1
    swap = [(i, i ^ 1) for i in range(count)]
    ahead = pairs(range(count // 2 - 1), 1, count)

    def send(x, route):
        return lax.ppermute(x, "head", route)

    own, own_a, own_b = collect(keys, values, segments, modality, place)
    params = gather_params(q_scale, q_shift, k_scale, k_shift)
    first = send(own, ahead)
    sources = range(count // 2 - 4)
    back_b = send(own_b, pairs(sources, -2, count))
    first_a, first_b = first[: 2 * ROWS], first[2 * ROWS :]
    first_a, back_b = lax.optimization_barrier((first_a, back_b))
    second_a = send(first_a, ahead)
    second_b = send(first_b, ahead)
    fourth_b = send(back_b, pairs([z - 2 for z in sources], -2, count))
    second_a, params = lax.optimization_barrier((second_a, params))
    third_a = send(second_a, ahead)
    third_b = send(second_b, ahead)
    fourth_a = send(third_a, ahead)

    def crossed(own, first, second, third, fourth):
        lacking = jnp.where(odd, fourth, own)
        return send(jnp.concatenate([first, second, third, lacking], axis=0), swap)

    all_b = [own_b, first_b, second_b, third_b, fourth_b]
    all_b.append(crossed(*all_b))
    all_a = [own_a, first_a, second_a, third_a, fourth_a]
    all_a.append(crossed(*all_a))
    out = attend(1, queries, all_b, all_b, params, None)
    return attend(0, queries, all_a, all_b, params, out)


def solution(mesh):
    rows = P("dp", "head", None)
    marks = P("dp", "head")
    norms = P(None, None, "dp")
    placed = (rows, rows, rows, marks, marks, norms, norms, norms, norms)
    return jax.shard_map(
        on_device, mesh=mesh, in_specs=placed, out_specs=rows, check_vma=False
    )
```

time: 83.5 us -> 77.5 us (0.928)
  the two profiles are of different devices: /device:TPU:195 before, /device:TPU:1 now
where the time goes in v2:
time: 77.5 us; the launch traced here: 77 us
  starting transfers between devices  50.3 us (65%)
  Pallas kernels  17.6 us (23%)
  waiting for transfers between devices  8.48 us (11%)
    ppermute x10, starting transfers between devices, send(): return lax.ppermute(x, 'head', route)  40.7 us
    pallas_call x2, Pallas kernels, attend(): pl.pallas_call(functools.partial(attend_kernel, pack, tuple(blocks)), gri...  14.1 us
    all_to_all x1, starting transfers between devices, gather_params(): whole = lax.all_to_all(sent, 'dp', split_axis=0, concat_axis=0, tiled=True)  9.67 us
    ppermute x10, waiting for transfers between devices, send(): return lax.ppermute(x, 'head', route)  8.48 us
    pallas_call x1, Pallas kernels, collect(): pl.pallas_call(collect_kernel, grid=(1,), in_specs=[pl.BlockSpec(memory_s...  2.06 us
  transfers between devices with their start and end apart: 11, of which 5 were waited for; matrix products, arithmetic and copies ran while one was open for 0% of the time, Pallas kernels for 11%

profile of v2, /device:TPU:1, one launch (start us, length us, event | category | flops | bytes accessed | tf_op | source)
XLA Modules:
  0.0 77.0 jit_solution(14880797382300171204)
XLA Ops:
  0.0 2.1 %collect.1 = (bf16[272,1024]{1,0:T(8,128)(2,1)}, bf16[128,1024]{1,0:T(8,128)(2,1)}, bf16[144,1024]{1,0:T(8,128)(2,1)}) custom-call(s32[1]{0:T(128)} %bitcast.place_ref, bf16[2,64,1024]{2,1,0:T(8,128)(2,1)} %keys_ref.1, bf16[2,64,1024]{2,1,0:T(8,128)(2,1)} %values_ref.1, s32[2,64]{1,0:T(2,128)} %segments_ref.1, s32[2,64]{1,0:T(2,128)} %modality_ref.1), custom_call_target="tpu_custom_call" | custom-call | tf_op jit(solution)/shard_map/collect/pallas_call | solution.py:165
  2.1 0.0 copy-start.1
  2.1 5.0 %collective-permute-start = (bf16[272,1024]{1,0:T(8,128)(2,1)}, bf16[272,1024]{1,0:T(8,128)(2,1)S(1)}, u32[]{:S(2)}, u32[]{:S(2)}) collective-permute-start(bf16[272,1024]{1,0:T(8,128)(2,1)} %get-tuple-element.13), channel_id=1, source_target_pairs={{0,2},{1,3},{2,4},{3,5},{4,6},{5,7},{6,8},{7,9},{8,10},{9,11},{10,... | collective-permute-start | bytes 1671176 | tf_op jit(solution)/shard_map/ppermute | solution.py:212
  7.0 9.7 %collective-permute-start.3 = (bf16[144,1024]{1,0:T(8,128)(2,1)}, bf16[144,1024]{1,0:T(8,128)(2,1)S(1)}, u32[]{:S(2)}, u32[]{:S(2)}) collective-permute-start(bf16[144,1024]{1,0:T(8,128)(2,1)} %get-tuple-element.12.refs_0_.refs_9_), channel_id=1, source_target_pairs={{0,12},{1,13},{2,14},{3,15},{4,0},{5,1},{6,2},{7,3},{16,28},{17,29... | collective-permute-start | bytes 884744 | tf_op jit(solution)/shard_map/ppermute | solution.py:212
  16.8 1.5 %spread.1 = f32[32,4,384]{2,1,0:T(4,128)} custom-call(f32[2,4,64]{2,1,0:T(4,128)} %bitcast.5, f32[2,4,64]{2,1,0:T(4,128)} %bitcast.6, f32[2,4,8]{2,1,0:T(4,128)} %bitcast.7, f32[2,4,8]{2,1,0:T(4,128)} %bitcast.8), custom_call_target="tpu_custom_call" | custom-call | tf_op jit(solution)/shard_map/spread/pallas_call | solution.py:191
  18.3 9.7 %all-to-all-start = ((f32[32,4,384]{2,1,0:T(4,128)}), f32[32,4,384]{2,1,0:T(4,128)S(1)}, u32[]{:S(2)}, u32[]{:S(2)}) async-start(f32[32,4,384]{2,1,0:T(4,128)} %spread.1), calls=%async_computation | async-start | bytes 393216 | tf_op jit(solution)/shard_map/all_to_all | solution.py:200
  28.0 0.0 collective-permute-done
  28.0 0.0 copy-start.2
  28.0 1.2 %collective-permute-done.3 = bf16[144,1024]{1,0:T(8,128)(2,1)S(1)} collective-permute-done((bf16[144,1024]{1,0:T(8,128)(2,1)}, bf16[144,1024]{1,0:T(8,128)(2,1)S(1)}, u32[]{:S(2)}, u32[]{:S(2)}) %collective-permute-start.3) | collective-permute-done | bytes 294944 | tf_op jit(solution)/shard_map/ppermute | solution.py:212
  29.2 1.3 %collective-permute-start.6 = (bf16[128,1024]{1,0:T(8,128)(2,1)S(1)}, bf16[128,1024]{1,0:T(8,128)(2,1)S(1)}, u32[]{:S(2)}, u32[]{:S(2)}) collective-permute-start(bf16[128,1024]{1,0:T(8,128)(2,1)S(1)} %slice.9.refs_10_), channel_id=1, source_target_pairs={{0,2},{1,3},{2,4},{3,5},{4,6},{5,7},{6,8},{7,9},{8,10},{9,11},{10,... | collective-permute-start | bytes 786440 | tf_op jit(solution)/shard_map/ppermute | solution.py:212
  30.6 1.3 %collective-permute-start.1 = (bf16[144,1024]{1,0:T(8,128)(2,1)S(1)}, bf16[144,1024]{1,0:T(8,128)(2,1)S(1)}, u32[]{:S(2)}, u32[]{:S(2)}) collective-permute-start(bf16[144,1024]{1,0:T(8,128)(2,1)S(1)} %slice.8.refs_1_.refs_10_), channel_id=1, source_target_pairs={{0,2},{1,3},{2,4},{3,5},{4,6},{5,7},{6,8},{7,9},{8,10},{9,11},{10,... | collective-permute-start | bytes 884744 | tf_op jit(solution)/shard_map/ppermute | solution.py:212
  31.9 7.4 %collective-permute-start.4 = (bf16[144,1024]{1,0:T(8,128)(2,1)S(1)}, bf16[144,1024]{1,0:T(8,128)(2,1)S(1)}, u32[]{:S(2)}, u32[]{:S(2)}) collective-permute-start(bf16[144,1024]{1,0:T(8,128)(2,1)S(1)} %collective-permute-done.3), channel_id=1, source_target_pairs={{12,8},{13,9},{14,10},{15,11},{0,12},{1,13},{2,14},{3,15},{28,24},... | collective-permute-start | bytes 884744 | tf_op jit(solution)/shard_map/ppermute | solution.py:212
  39.2 0.0 all-to-all-done
  39.2 0.1 reshape.7.refs_15_
  39.3 0.0 collective-permute-done.6.refs_11_
  39.3 1.3 %collective-permute-start.7 = (bf16[128,1024]{1,0:T(8,128)(2,1)S(1)}, bf16[128,1024]{1,0:T(8,128)(2,1)S(1)}, u32[]{:S(2)}, u32[]{:S(2)}) collective-permute-start(bf16[128,1024]{1,0:T(8,128)(2,1)S(1)} %collective-permute-done.6.refs_11_), channel_id=1, source_target_pairs={{0,2},{1,3},{2,4},{3,5},{4,6},{5,7},{6,8},{7,9},{8,10},{9,11},{10,... | collective-permute-start | bytes 786440 | tf_op jit(solution)/shard_map/ppermute | solution.py:212
  40.6 1.7 %collective-permute-done.1.refs_2_.refs_11_ = bf16[144,1024]{1,0:T(8,128)(2,1)S(1)} collective-permute-done((bf16[144,1024]{1,0:T(8,128)(2,1)S(1)}, bf16[144,1024]{1,0:T(8,128)(2,1)S(1)}, u32[]{:S(2)}, u32[]{:S(2)}) %collective-permute-start.1) | collective-permute-done | bytes 294944 | tf_op jit(solution)/shard_map/ppermute | solution.py:212
  42.3 4.1 %collective-permute-start.2 = (bf16[144,1024]{1,0:T(8,128)(2,1)S(1)}, bf16[144,1024]{1,0:T(8,128)(2,1)S(1)}, u32[]{:S(2)}, u32[]{:S(2)}) collective-permute-start(bf16[144,1024]{1,0:T(8,128)(2,1)S(1)} %collective-permute-done.1.refs_2_.refs_11_), channel_id=1, source_target_pairs={{0,2},{1,3},{2,4},{3,5},{4,6},{5,7},{6,8},{7,9},{8,10},{9,11},{10,... | collective-permute-start | bytes 884744 | tf_op jit(solution)/shard_map/ppermute | solution.py:212
  46.4 1.5 %collective-permute-done.7.refs_12_ = bf16[128,1024]{1,0:T(8,128)(2,1)S(1)} collective-permute-done((bf16[128,1024]{1,0:T(8,128)(2,1)S(1)}, bf16[128,1024]{1,0:T(8,128)(2,1)S(1)}, u32[]{:S(2)}, u32[]{:S(2)}) %collective-permute-start.7) | collective-permute-done | bytes 262176 | tf_op jit(solution)/shard_map/ppermute | solution.py:212
  47.9 4.1 %collective-permute-start.8 = (bf16[128,1024]{1,0:T(8,128)(2,1)S(1)}, bf16[128,1024]{1,0:T(8,128)(2,1)S(1)}, u32[]{:S(2)}, u32[]{:S(2)}) collective-permute-start(bf16[128,1024]{1,0:T(8,128)(2,1)S(1)} %collective-permute-done.7.refs_12_), channel_id=1, source_target_pairs={{0,2},{1,3},{2,4},{3,5},{4,6},{5,7},{6,8},{7,9},{8,10},{9,11},{10,... | collective-permute-start | bytes 786440 | tf_op jit(solution)/shard_map/ppermute | solution.py:212
  52.1 0.0 collective-permute-done.4.refs_4_.refs_13_
  52.1 0.0 copy-done.1
  52.1 0.0 copy-start
  52.1 2.1 %collective-permute-done.2.refs_3_.refs_12_ = bf16[144,1024]{1,0:T(8,128)(2,1)S(1)} collective-permute-done((bf16[144,1024]{1,0:T(8,128)(2,1)S(1)}, bf16[144,1024]{1,0:T(8,128)(2,1)S(1)}, u32[]{:S(2)}, u32[]{:S(2)}) %collective-permute-start.2) | collective-permute-done | bytes 294944 | tf_op jit(solution)/shard_map/ppermute | solution.py:212
  54.3 0.1 pad_maximum_fusion
  54.3 3.5 %collective-permute-start.5 = (bf16[576,1024]{1,0:T(8,128)(2,1)S(1)}, bf16[576,1024]{1,0:T(8,128)(2,1)S(1)}, u32[]{:S(2)}, u32[]{:S(2)}) collective-permute-start(bf16[576,1024]{1,0:T(8,128)(2,1)S(1)} %pad_maximum_fusion), channel_id=1, source_target_pairs={{0,1},{1,0},{2,3},{3,2},{4,5},{5,4},{6,7},{7,6},{8,9},{9,8},{10,11... | collective-permute-start | bytes 3538952 | tf_op jit(solution)/shard_map/ppermute | solution.py:212
  57.9 2.0 %collective-permute-done.8.refs_13_ = bf16[128,1024]{1,0:T(8,128)(2,1)S(1)} collective-permute-done((bf16[128,1024]{1,0:T(8,128)(2,1)S(1)}, bf16[128,1024]{1,0:T(8,128)(2,1)S(1)}, u32[]{:S(2)}, u32[]{:S(2)}) %collective-permute-start.8) | collective-permute-done | bytes 262176 | tf_op jit(solution)/shard_map/ppermute | solution.py:212
  59.9 0.0 copy-done.2
  59.9 0.1 pad_maximum_fusion.1
  60.0 2.9 %collective-permute-start.9 = (bf16[512,1024]{1,0:T(8,128)(2,1)S(1)}, bf16[512,1024]{1,0:T(8,128)(2,1)S(1)}, u32[]{:S(2)}, u32[]{:S(2)}) collective-permute-start(bf16[512,1024]{1,0:T(8,128)(2,1)S(1)} %pad_maximum_fusion.1), channel_id=1, source_target_pairs={{0,1},{1,0},{2,3},{3,2},{4,5},{5,4},{6,7},{7,6},{8,9},{9,8},{10,11... | collective-permute-start | bytes 3145736 | tf_op jit(solution)/shard_map/ppermute | solution.py:212
  62.9 0.0 collective-permute-done.5.refs_5_.refs_6_.refs_7_.refs_8_.refs_14_
  62.9 0.0 copy-done
  62.9 7.0 %attend.2.refs_16_ = bf16[2,64,8192]{2,1,0:T(8,128)(2,1)} custom-call(bf16[2,64,8192]{2,1,0:T(8,128)(2,1)S(1)} %copy-done, bf16[144,1024]{1,0:T(8,128)(2,1)S(1)} %copy-done.1, bf16[144,1024]{1,0:T(8,128)(2,1)S(1)} %slice.8.refs_1_.refs_10_, bf16[144,1024]{1,0:T(8,128)(2,1)S(1)} %collective-permute-done.1.refs_2_.refs_11_, ...), custom_call_target="tpu_custom_call" | custom-call | flops 1811939328 | bytes 4456448 | tf_op jit(solution)/shard_map/attend/pallas_call | solution.py:118
  70.0 0.0 collective-permute-done.9.refs_14_
  70.0 7.0 %attend.3 = bf16[2,64,8192]{2,1,0:T(8,128)(2,1)} custom-call(bf16[2,64,8192]{2,1,0:T(8,128)(2,1)S(1)} %copy-done, bf16[144,1024]{1,0:T(8,128)(2,1)S(1)} %copy-done.1, bf16[144,1024]{1,0:T(8,128)(2,1)S(1)} %slice.8.refs_1_.refs_10_, bf16[144,1024]{1,0:T(8,128)(2,1)S(1)} %collective-permute-done.1.refs_2_.refs_11_, ...), custom_call_target="tpu_custom_call", output_to_operand_aliasing={{}: (17, {})} | custom-call | flops 1811939328 | bytes 4456448 | tf_op jit(solution)/shard_map/attend/pallas_call | solution.py:118
  (4 shorter events, 0.1 us)
Async XLA Ops:
  2.1 50.0 %copy-start.1 = (bf16[144,1024]{1,0:T(8,128)(2,1)S(1)}, bf16[144,1024]{1,0:T(8,128)(2,1)}, u32[]{:S(2)}) copy-start(bf16[144,1024]{1,0:T(8,128)(2,1)} %get-tuple-element.12.refs_0_.refs_9_) | copy-start | bytes 884740
  2.1 25.9 %collective-permute-start = (bf16[272,1024]{1,0:T(8,128)(2,1)}, bf16[272,1024]{1,0:T(8,128)(2,1)S(1)}, u32[]{:S(2)}, u32[]{:S(2)}) collective-permute-start(bf16[272,1024]{1,0:T(8,128)(2,1)} %get-tuple-element.13), channel_id=1, source_target_pairs={{0,2},{1,3},{2,4},{3,5},{4,6},{5,7},{6,8},{7,9},{8,10},{9,11},{10,... | collective-permute-start | bytes 1671176 | tf_op jit(solution)/shard_map/ppermute | solution.py:212
  7.0 22.2 %collective-permute-start.3 = (bf16[144,1024]{1,0:T(8,128)(2,1)}, bf16[144,1024]{1,0:T(8,128)(2,1)S(1)}, u32[]{:S(2)}, u32[]{:S(2)}) collective-permute-start(bf16[144,1024]{1,0:T(8,128)(2,1)} %get-tuple-element.12.refs_0_.refs_9_), channel_id=1, source_target_pairs={{0,12},{1,13},{2,14},{3,15},{4,0},{5,1},{6,2},{7,3},{16,28},{17,29... | collective-permute-start | bytes 884744 | tf_op jit(solution)/shard_map/ppermute | solution.py:212
  18.3 20.9 %all-to-all-start = ((f32[32,4,384]{2,1,0:T(4,128)}), f32[32,4,384]{2,1,0:T(4,128)S(1)}, u32[]{:S(2)}, u32[]{:S(2)}) async-start(f32[32,4,384]{2,1,0:T(4,128)} %spread.1), calls=%async_computation | async-start | bytes 393216 | tf_op jit(solution)/shard_map/all_to_all | solution.py:200
  28.0 31.9 %copy-start.2 = (bf16[128,1024]{1,0:T(8,128)(2,1)S(1)}, bf16[128,1024]{1,0:T(8,128)(2,1)}, u32[]{:S(2)}) copy-start(bf16[128,1024]{1,0:T(8,128)(2,1)} %get-tuple-element.15.refs_9_) | copy-start | bytes 786436
  29.2 10.1 %collective-permute-start.6 = (bf16[128,1024]{1,0:T(8,128)(2,1)S(1)}, bf16[128,1024]{1,0:T(8,128)(2,1)S(1)}, u32[]{:S(2)}, u32[]{:S(2)}) collective-permute-start(bf16[128,1024]{1,0:T(8,128)(2,1)S(1)} %slice.9.refs_10_), channel_id=1, source_target_pairs={{0,2},{1,3},{2,4},{3,5},{4,6},{5,7},{6,8},{7,9},{8,10},{9,11},{10,... | collective-permute-start | bytes 786440 | tf_op jit(solution)/shard_map/ppermute | solution.py:212
  30.6 11.8 %collective-permute-start.1 = (bf16[144,1024]{1,0:T(8,128)(2,1)S(1)}, bf16[144,1024]{1,0:T(8,128)(2,1)S(1)}, u32[]{:S(2)}, u32[]{:S(2)}) collective-permute-start(bf16[144,1024]{1,0:T(8,128)(2,1)S(1)} %slice.8.refs_1_.refs_10_), channel_id=1, source_target_pairs={{0,2},{1,3},{2,4},{3,5},{4,6},{5,7},{6,8},{7,9},{8,10},{9,11},{10,... | collective-permute-start | bytes 884744 | tf_op jit(solution)/shard_map/ppermute | solution.py:212
  31.9 20.2 %collective-permute-start.4 = (bf16[144,1024]{1,0:T(8,128)(2,1)S(1)}, bf16[144,1024]{1,0:T(8,128)(2,1)S(1)}, u32[]{:S(2)}, u32[]{:S(2)}) collective-permute-start(bf16[144,1024]{1,0:T(8,128)(2,1)S(1)} %collective-permute-done.3), channel_id=1, source_target_pairs={{12,8},{13,9},{14,10},{15,11},{0,12},{1,13},{2,14},{3,15},{28,24},... | collective-permute-start | bytes 884744 | tf_op jit(solution)/shard_map/ppermute | solution.py:212
  39.3 8.6 %collective-permute-start.7 = (bf16[128,1024]{1,0:T(8,128)(2,1)S(1)}, bf16[128,1024]{1,0:T(8,128)(2,1)S(1)}, u32[]{:S(2)}, u32[]{:S(2)}) collective-permute-start(bf16[128,1024]{1,0:T(8,128)(2,1)S(1)} %collective-permute-done.6.refs_11_), channel_id=1, source_target_pairs={{0,2},{1,3},{2,4},{3,5},{4,6},{5,7},{6,8},{7,9},{8,10},{9,11},{10,... | collective-permute-start | bytes 786440 | tf_op jit(solution)/shard_map/ppermute | solution.py:212
  42.3 11.9 %collective-permute-start.2 = (bf16[144,1024]{1,0:T(8,128)(2,1)S(1)}, bf16[144,1024]{1,0:T(8,128)(2,1)S(1)}, u32[]{:S(2)}, u32[]{:S(2)}) collective-permute-start(bf16[144,1024]{1,0:T(8,128)(2,1)S(1)} %collective-permute-done.1.refs_2_.refs_11_), channel_id=1, source_target_pairs={{0,2},{1,3},{2,4},{3,5},{4,6},{5,7},{6,8},{7,9},{8,10},{9,11},{10,... | collective-permute-start | bytes 884744 | tf_op jit(solution)/shard_map/ppermute | solution.py:212
  47.9 11.9 %collective-permute-start.8 = (bf16[128,1024]{1,0:T(8,128)(2,1)S(1)}, bf16[128,1024]{1,0:T(8,128)(2,1)S(1)}, u32[]{:S(2)}, u32[]{:S(2)}) collective-permute-start(bf16[128,1024]{1,0:T(8,128)(2,1)S(1)} %collective-permute-done.7.refs_12_), channel_id=1, source_target_pairs={{0,2},{1,3},{2,4},{3,5},{4,6},{5,7},{6,8},{7,9},{8,10},{9,11},{10,... | collective-permute-start | bytes 786440 | tf_op jit(solution)/shard_map/ppermute | solution.py:212
  52.1 10.8 %copy-start = (bf16[2,64,8192]{2,1,0:T(8,128)(2,1)S(1)}, bf16[2,64,8192]{2,1,0:T(8,128)(2,1)}, u32[]{:S(2)}) copy-start(bf16[2,64,8192]{2,1,0:T(8,128)(2,1)} %q_ref.3) | copy-start | bytes 6291460
  54.3 8.6 %collective-permute-start.5 = (bf16[576,1024]{1,0:T(8,128)(2,1)S(1)}, bf16[576,1024]{1,0:T(8,128)(2,1)S(1)}, u32[]{:S(2)}, u32[]{:S(2)}) collective-permute-start(bf16[576,1024]{1,0:T(8,128)(2,1)S(1)} %pad_maximum_fusion), channel_id=1, source_target_pairs={{0,1},{1,0},{2,3},{3,2},{4,5},{5,4},{6,7},{7,6},{8,9},{9,8},{10,11... | collective-permute-start | bytes 3538952 | tf_op jit(solution)/shard_map/ppermute | solution.py:212
  60.0 10.0 %collective-permute-start.9 = (bf16[512,1024]{1,0:T(8,128)(2,1)S(1)}, bf16[512,1024]{1,0:T(8,128)(2,1)S(1)}, u32[]{:S(2)}, u32[]{:S(2)}) collective-permute-start(bf16[512,1024]{1,0:T(8,128)(2,1)S(1)} %pad_maximum_fusion.1), channel_id=1, source_target_pairs={{0,1},{1,0},{2,3},{3,2},{4,5},{5,4},{6,7},{7,6},{8,9},{9,8},{10,11... | collective-permute-start | bytes 3145736 | tf_op jit(solution)/shard_map/ppermute | solution.py:212

commit v3 on v2

--- a/solution.py
+++ b/solution.py
@@ -206,25 +206,27 @@
     place = lax.axis_index("head")
     odd = place % 2 == 1
     swap = [(i, i ^ 1) for i in range(count)]
-    ahead = pairs(range(count // 2 - 1), 1, count)
+
+    def ahead(hop):
+        return pairs(range(hop - 1, count // 2 - 1), 1, count)
 
     def send(x, route):
         return lax.ppermute(x, "head", route)
 
     own, own_a, own_b = collect(keys, values, segments, modality, place)
     params = gather_params(q_scale, q_shift, k_scale, k_shift)
-    first = send(own, ahead)
+    first = send(own, ahead(1))
     sources = range(count // 2 - 4)
     back_b = send(own_b, pairs(sources, -2, count))
     first_a, first_b = first[: 2 * ROWS], first[2 * ROWS :]
     first_a, back_b = lax.optimization_barrier((first_a, back_b))
-    second_a = send(first_a, ahead)
-    second_b = send(first_b, ahead)
+    second_a = send(first_a, ahead(2))
+    second_b = send(first_b, ahead(2))
     fourth_b = send(back_b, pairs([z - 2 for z in sources], -2, count))
     second_a, params = lax.optimization_barrier((second_a, params))
-    third_a = send(second_a, ahead)
-    third_b = send(second_b, ahead)
-    fourth_a = send(third_a, ahead)
+    third_a = send(second_a, ahead(3))
+    third_b = send(second_b, ahead(3))
+    fourth_a = send(third_a, ahead(4))
 
     def crossed(own, first, second, third, fourth):
         lacking = jnp.where(odd, fourth, own)

time: 77.5 us -> 74.9 us (0.966)
  the two profiles are of different devices: /device:TPU:1 before, /device:TPU:445 now
where the time goes in v3:
time: 74.9 us; the launch traced here: 74.5 us
  starting transfers between devices  35.9 us (48%)
  waiting for transfers between devices  20.3 us (27%)
  Pallas kernels  17.6 us (23%)
    ppermute x10, starting transfers between devices, send(): return lax.ppermute(x, 'head', route)  27 us
    ppermute x10, waiting for transfers between devices, send(): return lax.ppermute(x, 'head', route)  20.3 us
    pallas_call x2, Pallas kernels, attend(): pl.pallas_call(functools.partial(attend_kernel, pack, tuple(blocks)), gri...  14.1 us
    all_to_all x1, starting transfers between devices, gather_params(): whole = lax.all_to_all(sent, 'dp', split_axis=0, concat_axis=0, tiled=True)  8.95 us
    pallas_call x1, Pallas kernels, collect(): pl.pallas_call(collect_kernel, grid=(1,), in_specs=[pl.BlockSpec(memory_s...  2.06 us
    pallas_call x1, Pallas kernels, gather_params(): pl.pallas_call(spread_kernel, grid=(1,), in_specs=[whole_block(x.shape) f...  1.51 us
  transfers between devices with their start and end apart: 11, of which 7 were waited for; matrix products, arithmetic and copies ran while one was open for 0% of the time, Pallas kernels for 11%

profile of v3, /device:TPU:445, one launch (start us, length us, event | category | flops | bytes accessed | tf_op | source)
XLA Modules:
  0.0 74.5 jit_solution(12124994501571996971)
XLA Ops:
  0.0 2.1 %collect.1 = (bf16[272,1024]{1,0:T(8,128)(2,1)}, bf16[128,1024]{1,0:T(8,128)(2,1)}, bf16[144,1024]{1,0:T(8,128)(2,1)}) custom-call(s32[1]{0:T(128)} %bitcast.place_ref, bf16[2,64,1024]{2,1,0:T(8,128)(2,1)} %keys_ref.1, bf16[2,64,1024]{2,1,0:T(8,128)(2,1)} %values_ref.1, s32[2,64]{1,0:T(2,128)} %segments_ref.1, s32[2,64]{1,0:T(2,128)} %modality_ref.1), custom_call_target="tpu_custom_call" | custom-call | tf_op jit(solution)/shard_map/collect/pallas_call | solution.py:165
  2.1 0.0 copy-start.1
  2.1 3.2 %collective-permute-start = (bf16[272,1024]{1,0:T(8,128)(2,1)}, bf16[272,1024]{1,0:T(8,128)(2,1)S(1)}, u32[]{:S(2)}, u32[]{:S(2)}) collective-permute-start(bf16[272,1024]{1,0:T(8,128)(2,1)} %get-tuple-element.13), channel_id=1, source_target_pairs={{0,2},{1,3},{2,4},{3,5},{4,6},{5,7},{6,8},{7,9},{8,10},{9,11},{10,... | collective-permute-start | bytes 1671176 | tf_op jit(solution)/shard_map/ppermute | solution.py:214
  5.3 1.3 %collective-permute-start.3 = (bf16[144,1024]{1,0:T(8,128)(2,1)}, bf16[144,1024]{1,0:T(8,128)(2,1)S(1)}, u32[]{:S(2)}, u32[]{:S(2)}) collective-permute-start(bf16[144,1024]{1,0:T(8,128)(2,1)} %get-tuple-element.12.refs_0_.refs_9_), channel_id=1, source_target_pairs={{0,12},{1,13},{2,14},{3,15},{4,0},{5,1},{6,2},{7,3},{16,28},{17,29... | collective-permute-start | bytes 884744 | tf_op jit(solution)/shard_map/ppermute | solution.py:214
  6.6 1.5 %spread.1 = f32[32,4,384]{2,1,0:T(4,128)} custom-call(f32[2,4,64]{2,1,0:T(4,128)} %bitcast.5, f32[2,4,64]{2,1,0:T(4,128)} %bitcast.6, f32[2,4,8]{2,1,0:T(4,128)} %bitcast.7, f32[2,4,8]{2,1,0:T(4,128)} %bitcast.8), custom_call_target="tpu_custom_call" | custom-call | tf_op jit(solution)/shard_map/spread/pallas_call | solution.py:191
  8.1 9.0 %all-to-all-start = ((f32[32,4,384]{2,1,0:T(4,128)}), f32[32,4,384]{2,1,0:T(4,128)S(1)}, u32[]{:S(2)}, u32[]{:S(2)}) async-start(f32[32,4,384]{2,1,0:T(4,128)} %spread.1), calls=%async_computation | async-start | bytes 393216 | tf_op jit(solution)/shard_map/all_to_all | solution.py:200
  17.1 0.7 collective-permute-done
  17.8 0.0 copy-start.2
  17.8 6.0 %collective-permute-done.3 = bf16[144,1024]{1,0:T(8,128)(2,1)S(1)} collective-permute-done((bf16[144,1024]{1,0:T(8,128)(2,1)}, bf16[144,1024]{1,0:T(8,128)(2,1)S(1)}, u32[]{:S(2)}, u32[]{:S(2)}) %collective-permute-start.3) | collective-permute-done | bytes 294944 | tf_op jit(solution)/shard_map/ppermute | solution.py:214
  23.9 1.9 %collective-permute-start.6 = (bf16[128,1024]{1,0:T(8,128)(2,1)S(1)}, bf16[128,1024]{1,0:T(8,128)(2,1)S(1)}, u32[]{:S(2)}, u32[]{:S(2)}) collective-permute-start(bf16[128,1024]{1,0:T(8,128)(2,1)S(1)} %slice.9.refs_10_), channel_id=1, source_target_pairs={{2,4},{3,5},{4,6},{5,7},{6,8},{7,9},{8,10},{9,11},{10,12},{11,13},... | collective-permute-start | bytes 786440 | tf_op jit(solution)/shard_map/ppermute | solution.py:214
  25.8 1.9 %collective-permute-start.1 = (bf16[144,1024]{1,0:T(8,128)(2,1)S(1)}, bf16[144,1024]{1,0:T(8,128)(2,1)S(1)}, u32[]{:S(2)}, u32[]{:S(2)}) collective-permute-start(bf16[144,1024]{1,0:T(8,128)(2,1)S(1)} %slice.8.refs_1_.refs_10_), channel_id=1, source_target_pairs={{2,4},{3,5},{4,6},{5,7},{6,8},{7,9},{8,10},{9,11},{10,12},{11,13},... | collective-permute-start | bytes 884744 | tf_op jit(solution)/shard_map/ppermute | solution.py:214
  27.7 4.5 %collective-permute-start.4 = (bf16[144,1024]{1,0:T(8,128)(2,1)S(1)}, bf16[144,1024]{1,0:T(8,128)(2,1)S(1)}, u32[]{:S(2)}, u32[]{:S(2)}) collective-permute-start(bf16[144,1024]{1,0:T(8,128)(2,1)S(1)} %collective-permute-done.3), channel_id=1, source_target_pairs={{12,8},{13,9},{14,10},{15,11},{0,12},{1,13},{2,14},{3,15},{28,24},... | collective-permute-start | bytes 884744 | tf_op jit(solution)/shard_map/ppermute | solution.py:214
  32.3 0.0 all-to-all-done
  32.3 0.1 reshape.7.refs_15_
  32.4 0.8 %collective-permute-done.6.refs_11_ = bf16[128,1024]{1,0:T(8,128)(2,1)S(1)} collective-permute-done((bf16[128,1024]{1,0:T(8,128)(2,1)S(1)}, bf16[128,1024]{1,0:T(8,128)(2,1)S(1)}, u32[]{:S(2)}, u32[]{:S(2)}) %collective-permute-start.6) | collective-permute-done | bytes 262176 | tf_op jit(solution)/shard_map/ppermute | solution.py:214
  33.1 2.2 %collective-permute-start.7 = (bf16[128,1024]{1,0:T(8,128)(2,1)S(1)}, bf16[128,1024]{1,0:T(8,128)(2,1)S(1)}, u32[]{:S(2)}, u32[]{:S(2)}) collective-permute-start(bf16[128,1024]{1,0:T(8,128)(2,1)S(1)} %collective-permute-done.6.refs_11_), channel_id=1, source_target_pairs={{4,6},{5,7},{6,8},{7,9},{8,10},{9,11},{10,12},{11,13},{12,14},{13,... | collective-permute-start | bytes 786440 | tf_op jit(solution)/shard_map/ppermute | solution.py:214
  35.4 4.1 %collective-permute-done.1.refs_2_.refs_11_ = bf16[144,1024]{1,0:T(8,128)(2,1)S(1)} collective-permute-done((bf16[144,1024]{1,0:T(8,128)(2,1)S(1)}, bf16[144,1024]{1,0:T(8,128)(2,1)S(1)}, u32[]{:S(2)}, u32[]{:S(2)}) %collective-permute-start.1) | collective-permute-done | bytes 294944 | tf_op jit(solution)/shard_map/ppermute | solution.py:214
  39.4 2.2 %collective-permute-start.2 = (bf16[144,1024]{1,0:T(8,128)(2,1)S(1)}, bf16[144,1024]{1,0:T(8,128)(2,1)S(1)}, u32[]{:S(2)}, u32[]{:S(2)}) collective-permute-start(bf16[144,1024]{1,0:T(8,128)(2,1)S(1)} %collective-permute-done.1.refs_2_.refs_11_), channel_id=1, source_target_pairs={{4,6},{5,7},{6,8},{7,9},{8,10},{9,11},{10,12},{11,13},{12,14},{13,... | collective-permute-start | bytes 884744 | tf_op jit(solution)/shard_map/ppermute | solution.py:214
  41.7 3.4 %collective-permute-done.7.refs_12_ = bf16[128,1024]{1,0:T(8,128)(2,1)S(1)} collective-permute-done((bf16[128,1024]{1,0:T(8,128)(2,1)S(1)}, bf16[128,1024]{1,0:T(8,128)(2,1)S(1)}, u32[]{:S(2)}, u32[]{:S(2)}) %collective-permute-start.7) | collective-permute-done | bytes 262176 | tf_op jit(solution)/shard_map/ppermute | solution.py:214
  45.1 2.2 %collective-permute-start.8 = (bf16[128,1024]{1,0:T(8,128)(2,1)S(1)}, bf16[128,1024]{1,0:T(8,128)(2,1)S(1)}, u32[]{:S(2)}, u32[]{:S(2)}) collective-permute-start(bf16[128,1024]{1,0:T(8,128)(2,1)S(1)} %collective-permute-done.7.refs_12_), channel_id=1, source_target_pairs={{6,8},{7,9},{8,10},{9,11},{10,12},{11,13},{12,14},{13,15},{22,24},... | collective-permute-start | bytes 786440 | tf_op jit(solution)/shard_map/ppermute | solution.py:214
  47.3 0.0 collective-permute-done.4.refs_4_.refs_13_
  47.3 0.0 copy-done.1
  47.4 0.0 copy-start
  47.4 4.0 %collective-permute-done.2.refs_3_.refs_12_ = bf16[144,1024]{1,0:T(8,128)(2,1)S(1)} collective-permute-done((bf16[144,1024]{1,0:T(8,128)(2,1)S(1)}, bf16[144,1024]{1,0:T(8,128)(2,1)S(1)}, u32[]{:S(2)}, u32[]{:S(2)}) %collective-permute-start.2) | collective-permute-done | bytes 294944 | tf_op jit(solution)/shard_map/ppermute | solution.py:214
  51.4 0.1 pad_maximum_fusion
  51.5 4.2 %collective-permute-start.5 = (bf16[576,1024]{1,0:T(8,128)(2,1)S(1)}, bf16[576,1024]{1,0:T(8,128)(2,1)S(1)}, u32[]{:S(2)}, u32[]{:S(2)}) collective-permute-start(bf16[576,1024]{1,0:T(8,128)(2,1)S(1)} %pad_maximum_fusion), channel_id=1, source_target_pairs={{0,1},{1,0},{2,3},{3,2},{4,5},{5,4},{6,7},{7,6},{8,9},{9,8},{10,11... | collective-permute-start | bytes 3538952 | tf_op jit(solution)/shard_map/ppermute | solution.py:214
  55.7 1.3 %collective-permute-done.8.refs_13_ = bf16[128,1024]{1,0:T(8,128)(2,1)S(1)} collective-permute-done((bf16[128,1024]{1,0:T(8,128)(2,1)S(1)}, bf16[128,1024]{1,0:T(8,128)(2,1)S(1)}, u32[]{:S(2)}, u32[]{:S(2)}) %collective-permute-start.8) | collective-permute-done | bytes 262176 | tf_op jit(solution)/shard_map/ppermute | solution.py:214
  57.0 0.0 copy-done.2
  57.0 0.1 pad_maximum_fusion.1
  57.1 3.2 %collective-permute-start.9 = (bf16[512,1024]{1,0:T(8,128)(2,1)S(1)}, bf16[512,1024]{1,0:T(8,128)(2,1)S(1)}, u32[]{:S(2)}, u32[]{:S(2)}) collective-permute-start(bf16[512,1024]{1,0:T(8,128)(2,1)S(1)} %pad_maximum_fusion.1), channel_id=1, source_target_pairs={{0,1},{1,0},{2,3},{3,2},{4,5},{5,4},{6,7},{7,6},{8,9},{9,8},{10,11... | collective-permute-start | bytes 3145736 | tf_op jit(solution)/shard_map/ppermute | solution.py:214
  60.4 0.0 collective-permute-done.5.refs_5_.refs_6_.refs_7_.refs_8_.refs_14_
  60.4 0.0 copy-done
  60.4 7.0 %attend.2.refs_16_ = bf16[2,64,8192]{2,1,0:T(8,128)(2,1)} custom-call(bf16[2,64,8192]{2,1,0:T(8,128)(2,1)S(1)} %copy-done, bf16[144,1024]{1,0:T(8,128)(2,1)S(1)} %copy-done.1, bf16[144,1024]{1,0:T(8,128)(2,1)S(1)} %slice.8.refs_1_.refs_10_, bf16[144,1024]{1,0:T(8,128)(2,1)S(1)} %collective-permute-done.1.refs_2_.refs_11_, ...), custom_call_target="tpu_custom_call" | custom-call | flops 1811939328 | bytes 4456448 | tf_op jit(solution)/shard_map/attend/pallas_call | solution.py:118
  67.4 0.0 collective-permute-done.9.refs_14_
  67.4 7.0 %attend.3 = bf16[2,64,8192]{2,1,0:T(8,128)(2,1)} custom-call(bf16[2,64,8192]{2,1,0:T(8,128)(2,1)S(1)} %copy-done, bf16[144,1024]{1,0:T(8,128)(2,1)S(1)} %copy-done.1, bf16[144,1024]{1,0:T(8,128)(2,1)S(1)} %slice.8.refs_1_.refs_10_, bf16[144,1024]{1,0:T(8,128)(2,1)S(1)} %collective-permute-done.1.refs_2_.refs_11_, ...), custom_call_target="tpu_custom_call", output_to_operand_aliasing={{}: (17, {})} | custom-call | flops 1811939328 | bytes 4456448 | tf_op jit(solution)/shard_map/attend/pallas_call | solution.py:118
  (4 shorter events, 0.1 us)
Async XLA Ops:
  2.1 45.2 %copy-start.1 = (bf16[144,1024]{1,0:T(8,128)(2,1)S(1)}, bf16[144,1024]{1,0:T(8,128)(2,1)}, u32[]{:S(2)}) copy-start(bf16[144,1024]{1,0:T(8,128)(2,1)} %get-tuple-element.12.refs_0_.refs_9_) | copy-start | bytes 884740
  2.1 15.7 %collective-permute-start = (bf16[272,1024]{1,0:T(8,128)(2,1)}, bf16[272,1024]{1,0:T(8,128)(2,1)S(1)}, u32[]{:S(2)}, u32[]{:S(2)}) collective-permute-start(bf16[272,1024]{1,0:T(8,128)(2,1)} %get-tuple-element.13), channel_id=1, source_target_pairs={{0,2},{1,3},{2,4},{3,5},{4,6},{5,7},{6,8},{7,9},{8,10},{9,11},{10,... | collective-permute-start | bytes 1671176 | tf_op jit(solution)/shard_map/ppermute | solution.py:214
  5.3 18.6 %collective-permute-start.3 = (bf16[144,1024]{1,0:T(8,128)(2,1)}, bf16[144,1024]{1,0:T(8,128)(2,1)S(1)}, u32[]{:S(2)}, u32[]{:S(2)}) collective-permute-start(bf16[144,1024]{1,0:T(8,128)(2,1)} %get-tuple-element.12.refs_0_.refs_9_), channel_id=1, source_target_pairs={{0,12},{1,13},{2,14},{3,15},{4,0},{5,1},{6,2},{7,3},{16,28},{17,29... | collective-permute-start | bytes 884744 | tf_op jit(solution)/shard_map/ppermute | solution.py:214
  8.1 24.2 %all-to-all-start = ((f32[32,4,384]{2,1,0:T(4,128)}), f32[32,4,384]{2,1,0:T(4,128)S(1)}, u32[]{:S(2)}, u32[]{:S(2)}) async-start(f32[32,4,384]{2,1,0:T(4,128)} %spread.1), calls=%async_computation | async-start | bytes 393216 | tf_op jit(solution)/shard_map/all_to_all | solution.py:200
  17.8 39.2 %copy-start.2 = (bf16[128,1024]{1,0:T(8,128)(2,1)S(1)}, bf16[128,1024]{1,0:T(8,128)(2,1)}, u32[]{:S(2)}) copy-start(bf16[128,1024]{1,0:T(8,128)(2,1)} %get-tuple-element.15.refs_9_) | copy-start | bytes 786436
  23.9 9.3 %collective-permute-start.6 = (bf16[128,1024]{1,0:T(8,128)(2,1)S(1)}, bf16[128,1024]{1,0:T(8,128)(2,1)S(1)}, u32[]{:S(2)}, u32[]{:S(2)}) collective-permute-start(bf16[128,1024]{1,0:T(8,128)(2,1)S(1)} %slice.9.refs_10_), channel_id=1, source_target_pairs={{2,4},{3,5},{4,6},{5,7},{6,8},{7,9},{8,10},{9,11},{10,12},{11,13},... | collective-permute-start | bytes 786440 | tf_op jit(solution)/shard_map/ppermute | solution.py:214
  25.8 13.6 %collective-permute-start.1 = (bf16[144,1024]{1,0:T(8,128)(2,1)S(1)}, bf16[144,1024]{1,0:T(8,128)(2,1)S(1)}, u32[]{:S(2)}, u32[]{:S(2)}) collective-permute-start(bf16[144,1024]{1,0:T(8,128)(2,1)S(1)} %slice.8.refs_1_.refs_10_), channel_id=1, source_target_pairs={{2,4},{3,5},{4,6},{5,7},{6,8},{7,9},{8,10},{9,11},{10,12},{11,13},... | collective-permute-start | bytes 884744 | tf_op jit(solution)/shard_map/ppermute | solution.py:214
  27.7 19.6 %collective-permute-start.4 = (bf16[144,1024]{1,0:T(8,128)(2,1)S(1)}, bf16[144,1024]{1,0:T(8,128)(2,1)S(1)}, u32[]{:S(2)}, u32[]{:S(2)}) collective-permute-start(bf16[144,1024]{1,0:T(8,128)(2,1)S(1)} %collective-permute-done.3), channel_id=1, source_target_pairs={{12,8},{13,9},{14,10},{15,11},{0,12},{1,13},{2,14},{3,15},{28,24},... | collective-permute-start | bytes 884744 | tf_op jit(solution)/shard_map/ppermute | solution.py:214
  33.1 11.9 %collective-permute-start.7 = (bf16[128,1024]{1,0:T(8,128)(2,1)S(1)}, bf16[128,1024]{1,0:T(8,128)(2,1)S(1)}, u32[]{:S(2)}, u32[]{:S(2)}) collective-permute-start(bf16[128,1024]{1,0:T(8,128)(2,1)S(1)} %collective-permute-done.6.refs_11_), channel_id=1, source_target_pairs={{4,6},{5,7},{6,8},{7,9},{8,10},{9,11},{10,12},{11,13},{12,14},{13,... | collective-permute-start | bytes 786440 | tf_op jit(solution)/shard_map/ppermute | solution.py:214
  39.4 11.9 %collective-permute-start.2 = (bf16[144,1024]{1,0:T(8,128)(2,1)S(1)}, bf16[144,1024]{1,0:T(8,128)(2,1)S(1)}, u32[]{:S(2)}, u32[]{:S(2)}) collective-permute-start(bf16[144,1024]{1,0:T(8,128)(2,1)S(1)} %collective-permute-done.1.refs_2_.refs_11_), channel_id=1, source_target_pairs={{4,6},{5,7},{6,8},{7,9},{8,10},{9,11},{10,12},{11,13},{12,14},{13,... | collective-permute-start | bytes 884744 | tf_op jit(solution)/shard_map/ppermute | solution.py:214
  45.1 11.9 %collective-permute-start.8 = (bf16[128,1024]{1,0:T(8,128)(2,1)S(1)}, bf16[128,1024]{1,0:T(8,128)(2,1)S(1)}, u32[]{:S(2)}, u32[]{:S(2)}) collective-permute-start(bf16[128,1024]{1,0:T(8,128)(2,1)S(1)} %collective-permute-done.7.refs_12_), channel_id=1, source_target_pairs={{6,8},{7,9},{8,10},{9,11},{10,12},{11,13},{12,14},{13,15},{22,24},... | collective-permute-start | bytes 786440 | tf_op jit(solution)/shard_map/ppermute | solution.py:214
  47.4 13.0 %copy-start = (bf16[2,64,8192]{2,1,0:T(8,128)(2,1)S(1)}, bf16[2,64,8192]{2,1,0:T(8,128)(2,1)}, u32[]{:S(2)}) copy-start(bf16[2,64,8192]{2,1,0:T(8,128)(2,1)} %q_ref.3) | copy-start | bytes 6291460
  51.5 8.9 %collective-permute-start.5 = (bf16[576,1024]{1,0:T(8,128)(2,1)S(1)}, bf16[576,1024]{1,0:T(8,128)(2,1)S(1)}, u32[]{:S(2)}, u32[]{:S(2)}) collective-permute-start(bf16[576,1024]{1,0:T(8,128)(2,1)S(1)} %pad_maximum_fusion), channel_id=1, source_target_pairs={{0,1},{1,0},{2,3},{3,2},{4,5},{5,4},{6,7},{7,6},{8,9},{9,8},{10,11... | collective-permute-start | bytes 3538952 | tf_op jit(solution)/shard_map/ppermute | solution.py:214
  57.1 10.3 %collective-permute-start.9 = (bf16[512,1024]{1,0:T(8,128)(2,1)S(1)}, bf16[512,1024]{1,0:T(8,128)(2,1)S(1)}, u32[]{:S(2)}, u32[]{:S(2)}) collective-permute-start(bf16[512,1024]{1,0:T(8,128)(2,1)S(1)} %pad_maximum_fusion.1), channel_id=1, source_target_pairs={{0,1},{1,0},{2,3},{3,2},{4,5},{5,4},{6,7},{7,6},{8,9},{9,8},{10,11... | collective-permute-start | bytes 3145736 | tf_op jit(solution)/shard_map/ppermute | solution.py:214
